TPU v7x, 256 devices: a whole 4x4x8 slice. The times are simulated.
256 devices in a mesh: dp: 64 (over z, y, core), expert: 4 (over x).
Axes of the slice: x: 4, y: 4, z: 8, core: 2. Of those that a mesh axis runs over, the one named last changes fastest.
Arguments:
- gradient: bfloat16 [4, 64, 64, 4096], P('expert', None, 'dp'), may hold values from -4000 to 4000
- second_moment: float32 [4, 64, 64, 4096], P('expert', None, 'dp'), may hold values from 0.1 to 10
- left_stat: float32 [4, 64, 512, 512], P('expert', 'dp'), may hold values from -4 to 4
- right_stat: float32 [4, 64, 512, 512], P('expert', 'dp'), may hold values from -4 to 4
- left_root: float32 [4, 64, 512, 512], P('expert', 'dp'), may hold values from -1 to 3
- right_root: float32 [4, 64, 512, 512], P('expert', 'dp'), may hold values from -1 to 3
- owner_table: int32 [4, 64], P('expert'), may hold values from 0 to 63, each once within a row
Outputs:
- update: bfloat16 [4, 64, 64, 4096], P('expert', None, 'dp')
- moment_new: float32 [4, 64, 64, 4096], P('expert', None, 'dp')
- left_new: float32 [4, 64, 512, 512], P('expert', 'dp')
- right_new: float32 [4, 64, 512, 512], P('expert', 'dp')
Inputs may be any that keep to these rules, and one draw needn't show every extreme that they name: Each row is a permutation; block b of expert e is held by dp index owner_table[e, b].
All inputs are finite; a program needn't handle non-finite values.
Results may differ from a plain program's by a relative error of at most 0.0049.
Values may be sent and summed in bfloat16 or wider, within the bound.
No kernel may reach another device: no remote copies, remote signals or barrier semaphores. Data moves between devices by JAX's collectives and lax.ppermute only.
A program may use at most 64 MiB of HBM per device.

v0:
```python
import math

import jax
import jax.numpy as jnp
from jax import lax
from jax.sharding import PartitionSpec as P

STAT_DECAY = 0.9
MOMENT_DECAY = 0.99
ADAM_EPS = 1e-08
NORM_EPS = 1e-06


def on_device(gradient, second_moment, left_stat, right_stat, left_root, right_root, owner_table):
    dp_count = lax.axis_size("dp")
    grad_rows = gradient[0, :, 0, :]
    local_rows, width = grad_rows.shape
    per_owner = left_stat.shape[1]
    block_size = left_stat.shape[-1]
    piece_rows = block_size // dp_count
    row_blocks = local_rows // piece_rows
    col_blocks = width // block_size
    total_blocks = row_blocks * col_blocks
    grad_wide = grad_rows.astype(jnp.float32)
    grad_sq = lax.psum(jnp.sum(grad_wide * grad_wide), ("dp", "expert"))
    norm_limit = math.sqrt(lax.axis_size("expert") * local_rows * dp_count * width)
    clip_factor = norm_limit / jnp.maximum(jnp.sqrt(grad_sq), norm_limit)
    clipped = clip_factor * grad_wide
    moment = MOMENT_DECAY * second_moment[0, :, 0, :] + (1.0 - MOMENT_DECAY) * clipped * clipped
    adam_dir = clipped / (jnp.sqrt(moment) + ADAM_EPS)
    adam_part = jnp.sum(
        (adam_dir * adam_dir).reshape(row_blocks, piece_rows, col_blocks, block_size), axis=(1, 3)
    ).reshape(total_blocks)
    owners = owner_table[0]
    block_of = (
        jnp.zeros((total_blocks,), jnp.int32)
        .at[owners]
        .set(jnp.arange(total_blocks, dtype=jnp.int32))
    )
    chosen = block_of.reshape(dp_count, per_owner).T
    grid_view = grad_rows.reshape(row_blocks, piece_rows, col_blocks, block_size)
    piece_index = jnp.arange(piece_rows, dtype=jnp.int32)[None, :, None]
    outgoing = grid_view[
        (chosen // col_blocks)[:, None, :], piece_index, (chosen % col_blocks)[:, None, :]
    ]
    arrived = lax.all_to_all(outgoing, "dp", split_axis=2, concat_axis=2, tiled=True)
    mine = arrived.reshape(per_owner, block_size, block_size)
    gram_weight = (1.0 - STAT_DECAY) * clip_factor * clip_factor / block_size
    left_new = STAT_DECAY * left_stat[0] + gram_weight * jnp.einsum(
        "sik,sjk->sij", mine, mine, preferred_element_type=jnp.float32
    )
    right_new = STAT_DECAY * right_stat[0] + gram_weight * jnp.einsum(
        "ski,skj->sij", mine, mine, preferred_element_type=jnp.float32
    )
    shampoo_f = jnp.einsum(
        "sij,sjk->sik", left_root[0], mine.astype(jnp.float32), precision=lax.Precision.HIGHEST
    )
    shampoo_f = jnp.einsum(
        "sij,sjk->sik", shampoo_f, right_root[0], precision=lax.Precision.HIGHEST
    )
    shampoo_sq = jnp.sum(shampoo_f * shampoo_f, axis=(1, 2))
    shampoo = shampoo_f.astype(jnp.bfloat16)
    my_slots = lax.axis_index("dp") * per_owner + jnp.arange(per_owner, dtype=jnp.int32)
    my_blocks = block_of[my_slots]
    back_shape = (per_owner, piece_rows, dp_count, block_size)
    adam_sq = lax.psum(adam_part, "dp")[my_blocks]
    graft_ratio = jnp.sqrt(adam_sq) / jnp.sqrt(shampoo_sq + NORM_EPS)
    kept = lax.optimization_barrier(shampoo)
    final = (graft_ratio[:, None, None] * kept.astype(jnp.float32)).astype(jnp.bfloat16)
    returned = lax.all_to_all(
        final.reshape(back_shape), "dp", split_axis=2, concat_axis=0, tiled=True
    )
    final_rows = returned[:, :, 0, :]
    placed = final_rows[owners.reshape(row_blocks, col_blocks)[:, None, :], piece_index]
    update = placed.reshape(local_rows, width)
    return (update[None, :, None, :], moment[None, :, None, :], left_new[None], right_new[None])


def solution(mesh):
    placed = (
        P("expert", None, "dp", None),
        P("expert", None, "dp", None),
        P("expert", "dp", None, None),
        P("expert", "dp", None, None),
        P("expert", "dp", None, None),
        P("expert", "dp", None, None),
        P("expert", None),
    )
    return jax.shard_map(
        on_device,
        mesh=mesh,
        in_specs=placed,
        out_specs=(
            P("expert", None, "dp", None),
            P("expert", None, "dp", None),
            P("expert", "dp", None, None),
            P("expert", "dp", None, None),
        ),
        check_vma=False,
    )
```

profile of v0, /device:TPU:1, one launch (start us, length us, event | category | flops | bytes accessed | tf_op | source)
XLA Modules:
  0.0 276.0 jit_solution(9795246004908716790)
XLA Ops:
  0.6 0.0 copy-start
  0.7 1.3 copy.41
  2.0 0.8 scatter_custom_fusion
  2.9 0.1 reshape.240
  2.9 4.3 %gather_fusion = bf16[512,512]{1,0:T(8,128)(2,1)S(1)} fusion(bf16[8,8,8,512]{3,2,1,0:T(8,128)(2,1)S(1)} %copy.41, s32[512]{0:T(512)S(1)} %reshape.240), kind=kCustom, calls=%fused_computation | custom fusion | bytes 1054720 | tf_op jit(solution)/shard_map/gather | solution.py:43
  7.2 1.1 copy.20
  8.3 13.3 %all-to-all-start = ((bf16[1,8,64,512]{3,1,0,2:T(8,128)(2,1)}), bf16[1,8,64,512]{3,1,0,2:T(8,128)(2,1)S(1)}, u32[]{:S(2)}, u32[]{:S(2)}) async-start(bf16[1,8,64,512]{3,1,0,2:T(8,128)(2,1)} %copy.20), calls=%async_computation | async-start | bytes 1048576 | tf_op jit(solution)/shard_map/all_to_all | solution.py:46
  21.6 2.8 multiply_reduce_fusion.1
  24.3 77.8 %psum.14 = f32[]{:T(128)} all-reduce(f32[]{:T(128)} %multiply_reduce_fusion.1), channel_id=1, replica_groups=mesh['dp'=64,'expert'=4] {'dp','expert'}, use_global_device_ids=true, to_apply=%region_1.0 | all-reduce | flops 1 | bytes 8 | tf_op jit(solution)/shard_map/psum | solution.py:25
  102.1 0.7 dynamic-slice.4
  104.9 7.2 %fusion.10 = (f32[1,64,1,4096]{3,2,1,0:T(1,128)}, f32[64,4096]{1,0:T(8,128)S(1)}) fusion(bf16[1,64,1,4096]{3,1,2,0:T(8,128)(2,1)S(1)} %copy-done.1, f32[1,64,1,4096]{3,2,1,0:T(1,128)S(1)} %copy-done.3, f32[]{:T(128)S(6)} %div.29), kind=kLoop, calls=%fused_computation.17 | loop fusion | flops 1572864 | bytes 3670020 | tf_op jit(solution)/shard_map/add | solution.py:29
  112.1 1.0 fusion.15
  113.1 0.1 reshape.190
  113.9 124.5 %psum.15 = f32[64]{0:T(128)S(1)} all-reduce(f32[64]{0:T(128)S(1)} %reshape.190), channel_id=1, replica_groups=mesh['dp'=64,'expert'=4] {'dp'}, use_global_device_ids=true, to_apply=%region_3.0 | all-reduce | flops 64 | bytes 512 | tf_op jit(solution)/shard_map/psum | solution.py:66
  238.5 0.6 dynamic-slice.5
  239.7 0.0 all-to-all-done
  239.8 0.2 copy.21
  239.9 1.2 fusion.13
  241.2 2.6 multiply_reduce_fusion
  244.4 0.1 multiply_convert_fusion
  244.5 1.1 copy.22
  245.6 7.7 %all-to-all-start.1 = ((bf16[1,8,64,512]{3,1,0,2:T(8,128)(2,1)}), bf16[1,8,64,512]{3,1,0,2:T(8,128)(2,1)S(1)}, u32[]{:S(2)}, u32[]{:S(2)}) async-start(bf16[1,8,64,512]{3,1,0,2:T(8,128)(2,1)} %copy.22), calls=%async_computation.1 | async-start | bytes 1048576 | tf_op jit(solution)/shard_map/all_to_all | solution.py:70
  253.4 0.5 broadcast.204
  253.9 0.7 reduce.8
  254.6 0.1 broadcast_in_dim_reshape_squeeze.3
  254.7 0.1 reshape.246
  254.8 0.0 copy-start.4
  254.8 2.8 fusion.4
  257.5 1.6 fusion.2
  259.1 12.0 %all-to-all-done.1 = bf16[1,8,64,512]{3,1,0,2:T(8,128)(2,1)S(1)} async-done(((bf16[1,8,64,512]{3,1,0,2:T(8,128)(2,1)}), bf16[1,8,64,512]{3,1,0,2:T(8,128)(2,1)S(1)}, u32[]{:S(2)}, u32[]{:S(2)}) %all-to-all-start.1) | async-done | bytes 524320 | tf_op jit(solution)/shard_map/all_to_all | solution.py:70
  271.1 3.8 %gather_fusion.1 = bf16[512,512]{1,0:T(8,128)(2,1)S(1)} fusion(bf16[64,8,512]{2,1,0:T(8,128)(2,1)S(1)} %bitcast.74, s32[512]{0:T(512)S(1)} %reshape.246), kind=kCustom, calls=%fused_computation.1 | custom fusion | bytes 1052672 | tf_op jit(solution)/shard_map/gather | solution.py:74
  274.9 1.0 broadcast_in_dim_reshape.3
  (20 shorter events, 0.1 us)
Async XLA Ops:
  0.6 240.5 %copy-start = (f32[1,1,512,512]{3,2,1,0:T(8,128)S(1)}, f32[1,1,512,512]{3,2,1,0:T(8,128)}, u32[]{:S(2)}) copy-start(f32[1,1,512,512]{3,2,1,0:T(8,128)} %param.12) | copy-start | bytes 3145732
  0.6 1.3 copy-start.5
  8.3 13.3 %copy-start.1 = (bf16[1,64,1,4096]{3,1,2,0:T(8,128)(2,1)S(1)}, bf16[1,64,1,4096]{3,1,2,0:T(8,128)(2,1)}, u32[]{:S(2)}) copy-start(bf16[1,64,1,4096]{3,1,2,0:T(8,128)(2,1)} %param.7) | copy-start | bytes 1572868
  8.3 96.6 %copy-start.3 = (f32[1,64,1,4096]{3,2,1,0:T(1,128)S(1)}, f32[1,64,1,4096]{3,2,1,0:T(1,128)}, u32[]{:S(2)}) copy-start(f32[1,64,1,4096]{3,2,1,0:T(1,128)} %param.8) | copy-start | bytes 3145732
  8.3 231.5 %all-to-all-start = ((bf16[1,8,64,512]{3,1,0,2:T(8,128)(2,1)}), bf16[1,8,64,512]{3,1,0,2:T(8,128)(2,1)S(1)}, u32[]{:S(2)}, u32[]{:S(2)}) async-start(bf16[1,8,64,512]{3,1,0,2:T(8,128)(2,1)} %copy.20), calls=%async_computation | async-start | bytes 1048576 | tf_op jit(solution)/shard_map/all_to_all | solution.py:46
  112.1 127.8 %copy-start.2 = (f32[1,1,512,512]{3,2,1,0:T(8,128)S(1)}, f32[1,1,512,512]{3,2,1,0:T(8,128)}, u32[]{:S(2)}) copy-start(f32[1,1,512,512]{3,2,1,0:T(8,128)} %param.11) | copy-start | bytes 3145732
  245.6 25.5 %all-to-all-start.1 = ((bf16[1,8,64,512]{3,1,0,2:T(8,128)(2,1)}), bf16[1,8,64,512]{3,1,0,2:T(8,128)(2,1)S(1)}, u32[]{:S(2)}, u32[]{:S(2)}) async-start(bf16[1,8,64,512]{3,1,0,2:T(8,128)(2,1)} %copy.22), calls=%async_computation.1 | async-start | bytes 1048576 | tf_op jit(solution)/shard_map/all_to_all | solution.py:70
  254.8 2.8 %copy-start.4 = (f32[1,1,512,512]{3,2,1,0:T(8,128)S(1)}, f32[1,1,512,512]{3,2,1,0:T(8,128)}, u32[]{:S(2)}) copy-start(f32[1,1,512,512]{3,2,1,0:T(8,128)} %param.10) | copy-start | bytes 3145732
where the time goes:
time: 277 us; the launch traced here: 276 us
  blocking collectives  202 us (73%)
  starting transfers between devices  21 us (8%)
  local copies, waits for them, and re-layouts  15.7 us (6%)
  waiting for transfers between devices  12 us (4%)
  other arithmetic  11.8 us (4%)
  matrix products  8.16 us (3%)
  between operations  5.05 us (2%)
    psum x1, blocking collectives, on_device(): adam_sq = lax.psum(adam_part, 'dp')[my_blocks]  125 us
    psum x1, blocking collectives, on_device(): grad_sq = lax.psum(jnp.sum(grad_wide * grad_wide), ('dp', 'expert'))  77.8 us
    all_to_all x1, starting transfers between devices, on_device(): lax.all_to_all(outgoing, 'dp', split_axis=2, concat_axis=2, tiled=True)  13.3 us
    all_to_all x1, waiting for transfers between devices, on_device(): lax.all_to_all(final.reshape(back_shape), 'dp', split_axis=2, concat_axis...  12 us
    all_to_all x1, starting transfers between devices, on_device(): lax.all_to_all(final.reshape(back_shape), 'dp', split_axis=2, concat_axis...  7.74 us
    add x1, other arithmetic, on_device(): MOMENT_DECAY * second_moment[0, :, 0, :]  7.22 us
  transfers between devices with their start and end apart: 2, of which 1 were waited for; matrix products, arithmetic and copies ran while one was open for 7% of the time, Pallas kernels for 0%

commit v1 on v0

v1 whole, which is shorter than its diff:
```python
import functools
import math

import jax
import jax.numpy as jnp
from jax import lax
from jax.experimental import pallas as pl
from jax.experimental.pallas import tpu as pltpu
from jax.sharding import PartitionSpec as P

STAT_DECAY = 0.9
MOMENT_DECAY = 0.99
ADAM_EPS = 1e-08
NORM_EPS = 1e-06
LANES = 128
SUB = 8
F32 = jnp.float32
BF16 = jnp.bfloat16
VMEM_LIMIT = 48 * 1024 * 1024


def call(body, out_shape, in_specs, out_specs, name, flops=0, moved=0, **kw):
    return pl.pallas_call(
        body,
        out_shape=out_shape,
        in_specs=in_specs,
        out_specs=out_specs,
        name=name,
        compiler_params=pltpu.CompilerParams(vmem_limit_bytes=VMEM_LIMIT),
        cost_estimate=pl.CostEstimate(flops=flops, bytes_accessed=moved, transcendentals=0),
        **kw,
    )


def vmem():
    return pl.BlockSpec(memory_space=pltpu.VMEM)


def smem():
    return pl.BlockSpec(memory_space=pltpu.SMEM)


def dot(a, b, ca=1, cb=0):
    return lax.dot_general(a, b, (((ca,), (cb,)), ((), ())), preferred_element_type=F32)


def split2(x):
    high = x.astype(BF16)
    return high, (x - high.astype(F32)).astype(BF16)


def spread(x):
    high = x.astype(BF16).astype(F32)
    rest = x - high
    mid = rest.astype(BF16).astype(F32)
    low = rest - mid
    row = lax.broadcasted_iota(jnp.int32, x.shape, 0)
    return jnp.where(row == 0, high, jnp.where(row == 1, mid, jnp.where(row == 2, low, 0.0))).astype(BF16)


def clip_of(grad_sq, limit):
    return limit / jnp.maximum(jnp.sqrt(grad_sq), limit)


def pack_kernel(row_blocks, col_blocks, block, owners, grad, out):
    total = jnp.zeros((SUB, block), F32)
    for pair in range(0, row_blocks, 2):
        for col in range(col_blocks):
            wide = grad[pair * SUB : (pair + 2) * SUB, col * block : (col + 1) * block].astype(F32)
            for half in range(2):
                piece = wide[half * SUB : (half + 1) * SUB]
                total += piece * piece
                out[owners[(pair + half) * col_blocks + col], :, :block] = piece.astype(BF16)
    tile = jnp.broadcast_to(jnp.sum(total, keepdims=True), (SUB, LANES))
    out[:, :, block:] = jnp.broadcast_to(spread(tile)[None], (out.shape[0], SUB, LANES))


def gather_sum_kernel(tiles, out):
    wide = tiles[...].astype(F32)
    out[...] = jnp.sum(jnp.sum(wide, axis=0), axis=0, keepdims=True)


def roots_kernel(dp, left, right, l_high, l_low, r_high, r_low):
    n = left.shape[0]
    row = lax.broadcasted_iota(jnp.int32, (n, n), 0)
    col = lax.broadcasted_iota(jnp.int32, (n, n), 1)
    per = n // dp
    order = (col == (row % per) * dp + row // per).astype(BF16)
    high, low = split2(left[...])
    for part, dest in ((high, l_high), (low, l_low)):
        rows = dot(order, part).astype(BF16)
        dest[...] = dot(rows, order, 1, 1).astype(BF16)
    r_high[...], r_low[...] = split2(right[...])


def left_kernel(l_high, l_low, arrived, piece, half):
    block = piece.shape[1]
    wide = arrived[:, :, :block].astype(F32).reshape(piece.shape)
    piece[...] = wide.astype(BF16)
    g = piece[...]
    half[...] = dot(l_high[...], g) + dot(l_low[...], g)


def right_kernel(half, r_high, r_low, out, norm):
    block = half.shape[1]
    high, low = split2(half[...])
    full = dot(high, r_high[...]) + dot(high, r_low[...]) + dot(low, r_high[...])
    norm[...] = jnp.broadcast_to(jnp.sum(full * full, keepdims=True), norm.shape)
    out[:, :, :block] = full.reshape(out.shape[0], SUB, block).astype(BF16)


def adam_kernel(limit, row_blocks, col_blocks, block, grad, second, sq_a, sq_b, norm, _, moment, tail, parts):
    clip = clip_of(sq_a[...] + sq_b[...], limit)
    chunks = block // LANES
    wide_chunks = col_blocks * chunks
    parts[...] = jnp.zeros_like(parts)
    for pair in range(0, row_blocks, 2):
        for col in range(col_blocks):
            sums = [jnp.zeros((SUB, LANES), F32) for _ in range(2)]
            for chunk in range(chunks):
                k = col * chunks + chunk
                wide = grad[pair * SUB : (pair + 2) * SUB, k * LANES : (k + 1) * LANES].astype(F32)
                for half in range(2):
                    clipped = clip * wide[half * SUB : (half + 1) * SUB]
                    place = pl.ds((pair + half) * SUB * wide_chunks + k, SUB, stride=wide_chunks)
                    new = MOMENT_DECAY * second[place, :] + (1.0 - MOMENT_DECAY) * clipped * clipped
                    moment[place, :] = new
                    adam = clipped / (jnp.sqrt(new) + ADAM_EPS)
                    sums[half] += adam * adam
            for half in range(2):
                b = (pair + half) * col_blocks + col
                parts[b : b + 1, :] = jnp.sum(sums[half], axis=0, keepdims=True)
    sums = lax.dot_general(
        jnp.ones((SUB, LANES), F32),
        parts[...],
        (((1,), (1,)), ((), ())),
        precision=lax.Precision.HIGHEST,
        preferred_element_type=F32,
    )
    lane = lax.broadcasted_iota(jnp.int32, (SUB, LANES), 1)
    tile = jnp.where(lane == row_blocks * col_blocks, norm[...], sums)
    tail[...] = jnp.broadcast_to(spread(tile)[None], tail.shape)


def gram_kernel(limit, dp, piece, left, right, sq_a, sq_b, left_new, right_new):
    n = piece.shape[0]
    clip = clip_of(sq_a[:, :1] + sq_b[:, :1], limit)
    weight = (1.0 - STAT_DECAY) * clip * clip / n
    row = lax.broadcasted_iota(jnp.int32, (n, n), 0)
    col = lax.broadcasted_iota(jnp.int32, (n, n), 1)
    per = n // dp
    order = (row == (col % per) * dp + col // per).astype(BF16)
    g = piece[...]
    right_new[...] = STAT_DECAY * right[...] + weight * dot(g, g, 0, 0)
    g = dot(order, g).astype(BF16)
    left_new[...] = STAT_DECAY * left[...] + weight * dot(g, g, 1, 1)


def place_kernel(row_blocks, col_blocks, block, owners, owner_lanes, returned, update):
    blocks = row_blocks * col_blocks
    tiles = jnp.sum(returned[:, :, block:].astype(F32), axis=1)
    adam_sq = jnp.sum(tiles, axis=0, keepdims=True)[:, :blocks]
    slot = lax.broadcasted_iota(jnp.int32, (tiles.shape[0], blocks), 0)
    norms = jnp.where(owner_lanes[...] == slot, tiles[:, blocks : blocks + 1], 0.0)
    norm_sq = jnp.sum(norms, axis=0, keepdims=True)
    ratio = jnp.sqrt(adam_sq) / jnp.sqrt(norm_sq + NORM_EPS)
    for pair in range(0, row_blocks, 2):
        for col in range(col_blocks):
            rows = []
            for half in range(2):
                b = (pair + half) * col_blocks + col
                rows.append(ratio[:, b : b + 1] * returned[owners[b], :, :block].astype(F32))
            update[pair * SUB : (pair + 2) * SUB, col * block : (col + 1) * block] = jnp.concatenate(
                rows, axis=0
            ).astype(BF16)


def on_device(gradient, second_moment, left_stat, right_stat, left_root, right_root, owner_table):
    dp = lax.axis_size("dp")
    experts = lax.axis_size("expert")
    _, local_rows, _, width = gradient.shape
    block = left_stat.shape[-1]
    row_blocks = local_rows // SUB
    col_blocks = width // block
    limit = math.sqrt(experts * local_rows * dp * width)
    grid = (row_blocks, col_blocks, block)
    grad = gradient.reshape(local_rows, width)
    second = second_moment.reshape(local_rows * width // LANES, LANES)
    owners = owner_table[0]
    packed = jax.ShapeDtypeStruct((dp, SUB, block + LANES), BF16)
    square = functools.partial(jax.ShapeDtypeStruct, (block, block))
    line = jax.ShapeDtypeStruct((1, LANES), F32)
    cube = 2 * block**3
    area = block * block

    def exchange(x):
        return lax.all_to_all(x, "dp", split_axis=0, concat_axis=0, tiled=True)

    outgoing = call(
        functools.partial(pack_kernel, *grid), packed, [smem(), vmem()], vmem(), "pack", moved=4 * area
    )(owners, grad)
    arrived = exchange(outgoing)
    l_high, l_low, r_high, r_low = call(
        functools.partial(roots_kernel, dp),
        (square(BF16),) * 4,
        [vmem()] * 2,
        (vmem(),) * 4,
        "roots",
        flops=4 * cube,
        moved=16 * area,
    )(left_root[0, 0], right_root[0, 0])
    tail = pl.BlockSpec((dp, SUB, LANES), lambda _: (0, 0, block // LANES))
    sq_a = call(gather_sum_kernel, line, [tail], vmem(), "norm", moved=area, grid=(1,))(arrived)
    sq_b = lax.ppermute(sq_a, "expert", [(j, j ^ 1) for j in range(experts)])
    piece, half = call(
        left_kernel, (square(BF16), square(F32)), [vmem()] * 3, (vmem(),) * 2, "left", flops=2 * cube, moved=12 * area
    )(l_high, l_low, arrived)
    sq_a = sq_a + sq_b
    sq_b = lax.ppermute(sq_a, "expert", [(j, j ^ 2) for j in range(experts)])
    ready, norm = call(
        right_kernel,
        (packed, jax.ShapeDtypeStruct((SUB, LANES), F32)),
        [vmem()] * 3,
        (vmem(),) * 2,
        "right",
        flops=3 * cube,
        moved=10 * area,
    )(half, r_high, r_low)
    moment, ready = call(
        functools.partial(adam_kernel, limit, *grid),
        (jax.ShapeDtypeStruct(second.shape, F32), packed),
        [vmem()] * 5 + [pl.BlockSpec(memory_space=pl.ANY)],
        (vmem(), tail),
        "adam",
        moved=10 * area,
        scratch_shapes=[pltpu.VMEM((LANES, LANES), F32)],
        input_output_aliases={5: 1},
        grid=(1,),
    )(grad, second, sq_a, sq_b, norm, ready)
    returned = exchange(ready)
    left_new, right_new = call(
        functools.partial(gram_kernel, limit, dp),
        (square(F32),) * 2,
        [vmem()] * 5,
        (vmem(),) * 2,
        "gram",
        flops=3 * cube,
        moved=18 * area,
    )(piece, left_stat[0, 0], right_stat[0, 0], sq_a, sq_b)
    update = call(
        functools.partial(place_kernel, *grid),
        jax.ShapeDtypeStruct((local_rows, width), BF16),
        [smem(), vmem(), vmem()],
        vmem(),
        "place",
        moved=4 * area,
    )(owners, owner_table, returned)
    return (
        update.reshape(gradient.shape),
        moment.reshape(second_moment.shape),
        left_new[None, None],
        right_new[None, None],
    )


def solution(mesh):
    rows = P("expert", None, "dp", None)
    slots = P("expert", "dp", None, None)
    return jax.shard_map(
        on_device,
        mesh=mesh,
        in_specs=(rows, rows, slots, slots, slots, slots, P("expert", None)),
        out_specs=(rows, rows, slots, slots),
        check_vma=False,
    )
```

time: 277 us -> 77.2 us (0.28)
  blocking collectives: 202 us -> 0 us
  waiting for transfers between devices: 12 us -> 33.9 us
  Pallas kernels: 0 us -> 12.1 us
  other arithmetic: 11.8 us -> 0.01 us
  local copies, waits for them, and re-layouts: 15.7 us -> 5.94 us
  matrix products: 8.16 us -> 0 us
  between operations: 5.05 us -> 0.76 us
  starting transfers between devices: 21 us -> 24.2 us
    psum x2 -> x0, blocking collectives: 202 us -> none  [the longest x1 125 us: on_device(): adam_sq = lax.psum(adam_part, 'dp')[my_blocks]]
    all_to_all x2, waiting for transfers between devices: 12 us -> 33.9 us  [exchange(): return lax.all_to_all(x, 'dp', split_axis=0, concat_axis=0, tiled=True)]
    pallas_call x0 -> x8, Pallas kernels: none -> 12.1 us  [the longest x1 2.58 us: on_device(): call(functools.partial(adam_kernel, limit, *grid), (jax.ShapeDtypeStruct(...]
    gather x5 -> x0, local copies, waits for them, and re-layouts: 10.4 us -> none  [the longest x2 5.34 us: on_device(): grid_view[(chosen // col_blocks)[:, None, :], piece_index, (chosen % col_...]
    dot_general x4 -> x0, matrix products: 8.16 us -> none  [the longest x1 2.75 us: on_device(): jnp.einsum('sik,sjk->sij', mine, mine, preferred_element_type=jnp.float32)]
    add x1, other arithmetic: 7.22 us -> 0.01 us  [on_device(): sq_a = sq_a + sq_b]
    unnamed x14 -> x32, local copies, waits for them, and re-layouts: 1.85 us -> 5.94 us
    ppermute x0 -> x2, starting transfers between devices: none -> 3.83 us  [the longest x1 2.54 us: on_device(): sq_b = lax.ppermute(sq_a, 'expert', [(j, j ^ 2) for j in range(experts)])]
  transfers between devices with their start and end apart: 2 -> 4, of which waited for: 1 -> 2; matrix products, arithmetic and copies ran while one was open for 7% -> 0% of each run, Pallas kernels for 0% -> 8%
where the time goes in v1:
time: 77.2 us; the launch traced here: 76.8 us
  waiting for transfers between devices  33.9 us (44%)
  starting transfers between devices  24.2 us (31%)
  Pallas kernels  12.1 us (16%)
  local copies, waits for them, and re-layouts  5.94 us (8%)
    all_to_all x2, waiting for transfers between devices, exchange(): return lax.all_to_all(x, 'dp', split_axis=0, concat_axis=0, tiled=True)  33.9 us
    all_to_all x2, starting transfers between devices, exchange(): return lax.all_to_all(x, 'dp', split_axis=0, concat_axis=0, tiled=True)  20.3 us
    unnamed x32, local copies, waits for them, and re-layouts  5.94 us
    pallas_call x1, Pallas kernels, on_device(): call(functools.partial(adam_kernel, limit, *grid), (jax.ShapeDtypeStruct(...  2.58 us
    ppermute x1, starting transfers between devices, on_device(): sq_b = lax.ppermute(sq_a, 'expert', [(j, j ^ 2) for j in range(experts)])  2.54 us
    pallas_call x1, Pallas kernels, on_device(): call(functools.partial(gram_kernel, limit, dp), (square(F32),) * 2, [vmem...  2.11 us
    pallas_call x1, Pallas kernels, on_device(): call(right_kernel, (packed, jax.ShapeDtypeStruct((SUB, LANES), F32)), [vm...  1.84 us
    pallas_call x1, Pallas kernels, on_device(): call(functools.partial(place_kernel, *grid), jax.ShapeDtypeStruct((local_...  1.68 us
  transfers between devices with their start and end apart: 4, of which 2 were waited for; matrix products, arithmetic and copies ran while one was open for 0% of the time, Pallas kernels for 8%

profile of v1, /device:TPU:1, one launch (start us, length us, event | category | flops | bytes accessed | tf_op | source)
XLA Modules:
  0.0 76.8 jit_solution(15308329390657601361)
XLA Ops:
  0.6 0.0 copy-start.3
  0.6 0.6 copy-done.3
  1.3 1.0 %copy-done = bf16[1,64,1,4096]{3,1,2,0:T(8,128)(2,1)S(1)} copy-done((bf16[1,64,1,4096]{3,1,2,0:T(8,128)(2,1)S(1)}, bf16[1,64,1,4096]{3,1,2,0:T(8,128)(2,1)}, u32[]{:S(2)}) %copy-start) | copy-done | bytes 524312
  2.3 1.6 %pack.1 = bf16[64,8,640]{2,1,0:T(8,128)(2,1)} custom-call(s32[64]{0:T(128)S(1)} %bitcast.14, bf16[64,4096]{1,0:T(8,128)(2,1)S(1)} %bitcast.11), custom_call_target="tpu_custom_call" | custom-call | bytes 1048576 | tf_op jit(solution)/shard_map/pack/pallas_call | solution.py:199
  3.9 13.2 %all-to-all-start = ((bf16[64,8,640]{2,1,0:T(8,128)(2,1)}), bf16[64,8,640]{2,1,0:T(8,128)(2,1)S(1)}, u32[]{:S(2)}, u32[]{:S(2)}) async-start(bf16[64,8,640]{2,1,0:T(8,128)(2,1)} %pack.1), calls=%async_computation | async-start | bytes 1310720 | tf_op jit(solution)/shard_map/all_to_all | solution.py:197
  17.1 0.0 copy-done.4
  17.1 0.0 copy-done.5
  17.1 1.5 %roots.1 = (bf16[512,512]{1,0:T(8,128)(2,1)S(1)}, bf16[512,512]{1,0:T(8,128)(2,1)S(1)}, bf16[512,512]{1,0:T(8,128)(2,1)S(1)}, bf16[512,512]{1,0:T(8,128)(2,1)S(1)}) custom-call(f32[512,512]{1,0:T(8,128)S(1)} %bitcast.16, f32[512,512]{1,0:T(8,128)S(1)} %bitcast.17), custom_call_target="tpu_custom_call" | custom-call | flops 1073741824 | bytes 4194304 | tf_op jit(solution)/shard_map/roots/pallas_call | solution.py:203
  18.6 0.0 copy-start.8
  18.6 0.8 %copy-done.8 = bf16[512,512]{1,0:T(8,128)(2,1)} copy-done((bf16[512,512]{1,0:T(8,128)(2,1)}, bf16[512,512]{1,0:T(8,128)(2,1)S(1)}, u32[]{:S(2)}) %copy-start.8) | copy-done | bytes 524312
  19.4 0.8 %copy-done.10 = bf16[512,512]{1,0:T(8,128)(2,1)} copy-done((bf16[512,512]{1,0:T(8,128)(2,1)}, bf16[512,512]{1,0:T(8,128)(2,1)S(1)}, u32[]{:S(2)}) %copy-start.10) | copy-done | bytes 524312
  20.2 0.8 %copy-done.12 = bf16[512,512]{1,0:T(8,128)(2,1)} copy-done((bf16[512,512]{1,0:T(8,128)(2,1)}, bf16[512,512]{1,0:T(8,128)(2,1)S(1)}, u32[]{:S(2)}) %copy-start.12) | copy-done | bytes 524312
  21.0 0.8 %copy-done.14 = bf16[512,512]{1,0:T(8,128)(2,1)} copy-done((bf16[512,512]{1,0:T(8,128)(2,1)}, bf16[512,512]{1,0:T(8,128)(2,1)S(1)}, u32[]{:S(2)}) %copy-start.14) | copy-done | bytes 524312
  21.8 15.6 %all-to-all-done.tiles.arrived = bf16[64,8,640]{2,1,0:T(8,128)(2,1)S(1)} async-done(((bf16[64,8,640]{2,1,0:T(8,128)(2,1)}), bf16[64,8,640]{2,1,0:T(8,128)(2,1)S(1)}, u32[]{:S(2)}, u32[]{:S(2)}) %all-to-all-start) | async-done | bytes 655392 | tf_op jit(solution)/shard_map/all_to_all | solution.py:197
  37.4 0.1 norm.1
  37.5 1.3 %collective-permute-start = (f32[1,128]{1,0:T(1,128)S(1)}, f32[1,128]{1,0:T(1,128)S(1)}, u32[]{:S(2)}, u32[]{:S(2)}) collective-permute-start(f32[1,128]{1,0:T(1,128)S(1)} %norm.1), channel_id=1, source_target_pairs={{0,1},{1,0},{2,3},{3,2},{4,5},{5,4},{6,7},{7,6},{8,9},{9,8},{10,11... | collective-permute-start | bytes 1544 | tf_op jit(solution)/shard_map/ppermute | solution.py:214
  38.8 0.0 copy-done.9
  38.8 1.0 %copy-done.11 = bf16[512,512]{1,0:T(8,128)(2,1)S(1)} copy-done((bf16[512,512]{1,0:T(8,128)(2,1)S(1)}, bf16[512,512]{1,0:T(8,128)(2,1)}, u32[]{:S(2)}) %copy-start.11) | copy-done | bytes 524312
  39.9 0.7 left.1
  40.6 0.0 collective-permute-done
  40.6 2.5 %collective-permute-start.1 = (f32[1,128]{1,0:T(1,128)S(1)}, f32[1,128]{1,0:T(1,128)S(1)}, u32[]{:S(2)}, u32[]{:S(2)}) collective-permute-start(f32[1,128]{1,0:T(1,128)S(1)} %add.3.sq_a), channel_id=1, source_target_pairs={{0,2},{1,3},{2,0},{3,1},{4,6},{5,7},{6,4},{7,5},{8,10},{9,11},{10,... | collective-permute-start | bytes 1544 | tf_op jit(solution)/shard_map/ppermute | solution.py:219
  43.1 0.0 copy-done.13
  43.1 0.0 copy-done.15
  43.1 1.8 %right.1 = (bf16[64,8,640]{2,1,0:T(8,128)(2,1)}, f32[8,128]{1,0:T(8,128)S(1)}) custom-call(f32[512,512]{1,0:T(8,128)S(1)} %get-tuple-element.18.half, bf16[512,512]{1,0:T(8,128)(2,1)S(1)} %copy-done.13, bf16[512,512]{1,0:T(8,128)(2,1)S(1)} %copy-done.15), custom_call_target="tpu_custom_call" | custom-call | flops 805306368 | bytes 2621440 | tf_op jit(solution)/shard_map/right/pallas_call | solution.py:220
  45.0 0.0 collective-permute-done.1.sq_b
  45.0 0.0 copy-done.2
  45.0 0.0 copy-start.7
  45.0 2.6 %adam.1 = (f32[2048,128]{1,0:T(8,128)}, bf16[64,8,640]{2,1,0:T(8,128)(2,1)}) custom-call(bf16[64,4096]{1,0:T(8,128)(2,1)S(1)} %bitcast.12, f32[2048,128]{1,0:T(8,128)S(1)} %bitcast.13, f32[1,128]{1,0:T(1,128)S(1)} %add.3.sq_a, f32[1,128]{1,0:T(1,128)S(1)} %collective-permute-done.1.sq_b, ...), custom_call_target="tpu_custom_call", output_to_operand_aliasing={{1}: (5, {})} | custom-call | bytes 2621440 | tf_op jit(solution)/shard_map/adam/pallas_call | solution.py:229
  47.6 7.2 %all-to-all-start.1 = ((bf16[64,8,640]{2,1,0:T(8,128)(2,1)}), bf16[64,8,640]{2,1,0:T(8,128)(2,1)S(1)}, u32[]{:S(2)}, u32[]{:S(2)}) async-start(bf16[64,8,640]{2,1,0:T(8,128)(2,1)} %get-tuple-element.23), calls=%async_computation.1 | async-start | bytes 1310720 | tf_op jit(solution)/shard_map/all_to_all | solution.py:197
  54.8 2.1 %gram.1 = (f32[512,512]{1,0:T(8,128)}, f32[512,512]{1,0:T(8,128)}) custom-call(bf16[512,512]{1,0:T(8,128)(2,1)S(1)} %get-tuple-element.25.piece, f32[512,512]{1,0:T(8,128)S(1)} %bitcast.18, f32[512,512]{1,0:T(8,128)S(1)} %bitcast.19, f32[1,128]{1,0:T(1,128)S(1)} %add.3.sq_a, f32[1,128]{1,0:T(1,128)S(1)} %collective-permute-done.1.sq_b), custom_call_target="tpu_custom_call" | custom-call | flops 805306368 | bytes 4718592 | tf_op jit(solution)/shard_map/gram/pallas_call | solution.py:241
  56.9 18.2 %all-to-all-done.1.returned = bf16[64,8,640]{2,1,0:T(8,128)(2,1)S(1)} async-done(((bf16[64,8,640]{2,1,0:T(8,128)(2,1)}), bf16[64,8,640]{2,1,0:T(8,128)(2,1)S(1)}, u32[]{:S(2)}, u32[]{:S(2)}) %all-to-all-start.1) | async-done | bytes 655392 | tf_op jit(solution)/shard_map/all_to_all | solution.py:197
  75.1 1.7 %place.1 = bf16[64,4096]{1,0:T(8,128)(2,1)} custom-call(s32[64]{0:T(128)S(1)} %bitcast.15, s32[1,64]{1,0:T(1,128)S(1)} %copy-done.3, bf16[64,8,640]{2,1,0:T(8,128)(2,1)S(1)} %all-to-all-done.1.returned), custom_call_target="tpu_custom_call" | custom-call | bytes 1048576 | tf_op jit(solution)/shard_map/place/pallas_call | solution.py:250
  (17 shorter events, 0.0 us)
Async XLA Ops:
  0.6 0.7 copy-start.3
  1.3 1.0 %copy-start = (bf16[1,64,1,4096]{3,1,2,0:T(8,128)(2,1)S(1)}, bf16[1,64,1,4096]{3,1,2,0:T(8,128)(2,1)}, u32[]{:S(2)}) copy-start(bf16[1,64,1,4096]{3,1,2,0:T(8,128)(2,1)} %param.7) | copy-start | bytes 1572868
  2.3 14.7 %copy-start.4 = (f32[1,1,512,512]{3,2,1,0:T(8,128)S(1)}, f32[1,1,512,512]{3,2,1,0:T(8,128)}, u32[]{:S(2)}) copy-start(f32[1,1,512,512]{3,2,1,0:T(8,128)} %param.11) | copy-start | bytes 3145732
  2.3 14.7 %copy-start.5 = (f32[1,1,512,512]{3,2,1,0:T(8,128)S(1)}, f32[1,1,512,512]{3,2,1,0:T(8,128)}, u32[]{:S(2)}) copy-start(f32[1,1,512,512]{3,2,1,0:T(8,128)} %param.12) | copy-start | bytes 3145732
  3.9 33.5 %all-to-all-start = ((bf16[64,8,640]{2,1,0:T(8,128)(2,1)}), bf16[64,8,640]{2,1,0:T(8,128)(2,1)S(1)}, u32[]{:S(2)}, u32[]{:S(2)}) async-start(bf16[64,8,640]{2,1,0:T(8,128)(2,1)} %pack.1), calls=%async_computation | async-start | bytes 1310720 | tf_op jit(solution)/shard_map/all_to_all | solution.py:197
  18.6 0.8 %copy-start.8 = (bf16[512,512]{1,0:T(8,128)(2,1)}, bf16[512,512]{1,0:T(8,128)(2,1)S(1)}, u32[]{:S(2)}) copy-start(bf16[512,512]{1,0:T(8,128)(2,1)S(1)} %get-tuple-element.16.l_high) | copy-start | bytes 1572868
  19.4 0.8 %copy-start.10 = (bf16[512,512]{1,0:T(8,128)(2,1)}, bf16[512,512]{1,0:T(8,128)(2,1)S(1)}, u32[]{:S(2)}) copy-start(bf16[512,512]{1,0:T(8,128)(2,1)S(1)} %get-tuple-element.17.l_low) | copy-start | bytes 1572868
  20.2 0.8 %copy-start.12 = (bf16[512,512]{1,0:T(8,128)(2,1)}, bf16[512,512]{1,0:T(8,128)(2,1)S(1)}, u32[]{:S(2)}) copy-start(bf16[512,512]{1,0:T(8,128)(2,1)S(1)} %get-tuple-element.19.r_high) | copy-start | bytes 1572868
  21.0 0.8 %copy-start.14 = (bf16[512,512]{1,0:T(8,128)(2,1)}, bf16[512,512]{1,0:T(8,128)(2,1)S(1)}, u32[]{:S(2)}) copy-start(bf16[512,512]{1,0:T(8,128)(2,1)S(1)} %get-tuple-element.20.r_low) | copy-start | bytes 1572868
  37.4 1.4 %copy-start.9 = (bf16[512,512]{1,0:T(8,128)(2,1)S(1)}, bf16[512,512]{1,0:T(8,128)(2,1)}, u32[]{:S(2)}) copy-start(bf16[512,512]{1,0:T(8,128)(2,1)} %copy-done.8) | copy-start | bytes 1572868
  37.5 3.1 %collective-permute-start = (f32[1,128]{1,0:T(1,128)S(1)}, f32[1,128]{1,0:T(1,128)S(1)}, u32[]{:S(2)}, u32[]{:S(2)}) collective-permute-start(f32[1,128]{1,0:T(1,128)S(1)} %norm.1), channel_id=1, source_target_pairs={{0,1},{1,0},{2,3},{3,2},{4,5},{5,4},{6,7},{7,6},{8,9},{9,8},{10,11... | collective-permute-start | bytes 1544 | tf_op jit(solution)/shard_map/ppermute | solution.py:214
  38.8 1.0 %copy-start.11 = (bf16[512,512]{1,0:T(8,128)(2,1)S(1)}, bf16[512,512]{1,0:T(8,128)(2,1)}, u32[]{:S(2)}) copy-start(bf16[512,512]{1,0:T(8,128)(2,1)} %copy-done.10) | copy-start | bytes 1572868
  39.9 3.3 %copy-start.13 = (bf16[512,512]{1,0:T(8,128)(2,1)S(1)}, bf16[512,512]{1,0:T(8,128)(2,1)}, u32[]{:S(2)}) copy-start(bf16[512,512]{1,0:T(8,128)(2,1)} %copy-done.12) | copy-start | bytes 1572868
  39.9 3.3 %copy-start.15 = (bf16[512,512]{1,0:T(8,128)(2,1)S(1)}, bf16[512,512]{1,0:T(8,128)(2,1)}, u32[]{:S(2)}) copy-start(bf16[512,512]{1,0:T(8,128)(2,1)} %copy-done.14) | copy-start | bytes 1572868
  40.6 4.4 %collective-permute-start.1 = (f32[1,128]{1,0:T(1,128)S(1)}, f32[1,128]{1,0:T(1,128)S(1)}, u32[]{:S(2)}, u32[]{:S(2)}) collective-permute-start(f32[1,128]{1,0:T(1,128)S(1)} %add.3.sq_a), channel_id=1, source_target_pairs={{0,2},{1,3},{2,0},{3,1},{4,6},{5,7},{6,4},{7,5},{8,10},{9,11},{10,... | collective-permute-start | bytes 1544 | tf_op jit(solution)/shard_map/ppermute | solution.py:219
  43.1 1.9 %copy-start.1 = (bf16[1,64,1,4096]{3,1,2,0:T(8,128)(2,1)S(1)}, bf16[1,64,1,4096]{3,1,2,0:T(8,128)(2,1)}, u32[]{:S(2)}) copy-start(bf16[1,64,1,4096]{3,1,2,0:T(8,128)(2,1)} %param.7) | copy-start | bytes 1572868
  43.1 1.9 %copy-start.2 = (f32[1,64,1,4096]{3,2,1,0:T(1,128)S(1)}, f32[1,64,1,4096]{3,2,1,0:T(1,128)}, u32[]{:S(2)}) copy-start(f32[1,64,1,4096]{3,2,1,0:T(1,128)} %param.8) | copy-start | bytes 3145732
  45.0 9.8 %copy-start.7 = (f32[1,1,512,512]{3,2,1,0:T(8,128)S(1)}, f32[1,1,512,512]{3,2,1,0:T(8,128)}, u32[]{:S(2)}) copy-start(f32[1,1,512,512]{3,2,1,0:T(8,128)} %param.10) | copy-start | bytes 3145732
  47.6 7.2 %copy-start.6 = (f32[1,1,512,512]{3,2,1,0:T(8,128)S(1)}, f32[1,1,512,512]{3,2,1,0:T(8,128)}, u32[]{:S(2)}) copy-start(f32[1,1,512,512]{3,2,1,0:T(8,128)} %param.9) | copy-start | bytes 3145732
  47.6 27.5 %all-to-all-start.1 = ((bf16[64,8,640]{2,1,0:T(8,128)(2,1)}), bf16[64,8,640]{2,1,0:T(8,128)(2,1)S(1)}, u32[]{:S(2)}, u32[]{:S(2)}) async-start(bf16[64,8,640]{2,1,0:T(8,128)(2,1)} %get-tuple-element.23), calls=%async_computation.1 | async-start | bytes 1310720 | tf_op jit(solution)/shard_map/all_to_all | solution.py:197

commit v2 on v1

v2 whole, which is shorter than its diff:
```python
import functools
import math

import jax
import jax.numpy as jnp
from jax import lax
from jax.experimental import pallas as pl
from jax.experimental.pallas import tpu as pltpu
from jax.sharding import PartitionSpec as P

STAT_DECAY = 0.9
MOMENT_DECAY = 0.99
ADAM_EPS = 1e-08
NORM_EPS = 1e-06
LANES = 128
SUB = 8
ROWS = 2
FOLDS = SUB // ROWS
F32 = jnp.float32
BF16 = jnp.bfloat16
VMEM_LIMIT = 48 * 1024 * 1024
PACK_LIMIT = 64 * 1024 * 1024 - 256 * 1024


def call(body, out_shape, in_specs, out_specs, name, flops=0, moved=0, limit=VMEM_LIMIT, **kw):
    return pl.pallas_call(
        body,
        out_shape=out_shape,
        in_specs=in_specs,
        out_specs=out_specs,
        name=name,
        compiler_params=pltpu.CompilerParams(vmem_limit_bytes=limit),
        cost_estimate=pl.CostEstimate(flops=flops, bytes_accessed=moved, transcendentals=0),
        **kw,
    )


def vmem():
    return pl.BlockSpec(memory_space=pltpu.VMEM)


def smem():
    return pl.BlockSpec(memory_space=pltpu.SMEM)


def hbm():
    return pl.BlockSpec(memory_space=pltpu.HBM)


def dot(a, b, ca=1, cb=0):
    return lax.dot_general(a, b, (((ca,), (cb,)), ((), ())), preferred_element_type=F32)


def split2(x):
    high = x.astype(BF16)
    return high, (x - high.astype(F32)).astype(BF16)


def spread(x):
    high = x.astype(BF16).astype(F32)
    row = lax.broadcasted_iota(jnp.int32, x.shape, 0)
    return jnp.where(row == 0, high, x - high).astype(BF16)


def fold(x):
    return jnp.concatenate([x[:, i * ROWS : (i + 1) * ROWS] for i in range(FOLDS)], axis=2).astype(BF16)


def unfold(x, block):
    return jnp.concatenate([x[:, :, i * block : (i + 1) * block].astype(F32) for i in range(FOLDS)], axis=1)


def clip_of(grad_sq, limit):
    return limit / jnp.maximum(jnp.sqrt(grad_sq), limit)


def pack_kernel(row_blocks, col_blocks, block, table, grad, out, owners, held, ready, sems, out_sems):
    rows = 2 * SUB
    place = pltpu.make_async_copy(table, owners, sems.at[row_blocks // 2])
    place.start()
    copies = []
    for pair in range(row_blocks // 2):
        span = pl.ds(pair * rows, rows)
        copies.append(pltpu.make_async_copy(grad.at[span], held.at[span], sems.at[pair]))
        copies[-1].start()
    place.wait()
    total = jnp.zeros((SUB, block), F32)
    for pair, copy in enumerate(copies):
        copy.wait()
        for col in range(col_blocks):
            wide = held[pair * rows : (pair + 1) * rows, col * block : (col + 1) * block].astype(F32)
            for side in range(2):
                piece = wide[side * SUB : (side + 1) * SUB]
                total += piece * piece
                slot = owners[0, (2 * pair + side) * col_blocks + col]
                ready[slot, :, : FOLDS * block] = fold(piece[None])[0]
                pltpu.make_async_copy(
                    ready.at[slot, :, : FOLDS * block], out.at[slot, :, : FOLDS * block], out_sems.at[0]
                ).start()
    tile = jnp.broadcast_to(jnp.sum(total, keepdims=True), (ROWS, LANES))
    ready[:, :, FOLDS * block :] = jnp.broadcast_to(spread(tile)[None], (ready.shape[0], ROWS, LANES))
    tails = pltpu.make_async_copy(ready.at[:, :, FOLDS * block :], out.at[:, :, FOLDS * block :], out_sems.at[1])
    tails.start()
    pltpu.make_async_copy(ready.at[:, :, : FOLDS * block], out.at[:, :, : FOLDS * block], out_sems.at[0]).wait()
    tails.wait()


def sum_kernel(tiles, out):
    wide = jnp.sum(tiles[...].astype(F32), axis=0)
    out[...] = jnp.sum(wide, axis=0, keepdims=True)


def roots_kernel(dp, left, right, l_parts, r_parts):
    n = left.shape[0]
    row = lax.broadcasted_iota(jnp.int32, (n, n), 0)
    col = lax.broadcasted_iota(jnp.int32, (n, n), 1)
    per = n // dp
    order = (col == (row % per) * dp + row // per).astype(BF16)
    for i, part in enumerate(split2(left[...])):
        rows = dot(order, part).astype(BF16)
        l_parts[i] = dot(rows, order, 1, 1).astype(BF16)
    r_parts[0], r_parts[1] = split2(right[...])


def arrived_block(block, arrived):
    return unfold(arrived, block).reshape(block, block).astype(BF16)


def left_kernel(block, l_parts, arrived, half):
    g = arrived_block(block, arrived)
    half[...] = dot(l_parts[0], g) + dot(l_parts[1], g)


def right_kernel(half, r_parts, out, norm):
    block = half.shape[1]
    high, low = split2(half[...])
    full = dot(high, r_parts[0]) + dot(high, r_parts[1]) + dot(low, r_parts[0])
    norm[...] = jnp.broadcast_to(jnp.sum(full * full, keepdims=True), norm.shape)
    out[:, :, : FOLDS * block] = fold(full.reshape(out.shape[0], SUB, block))


def adam_kernel(limit, row_blocks, col_blocks, block, grad, second, sq_a, sq_b, norm, _, tail, parts):
    clip = clip_of(sq_a[...] + sq_b[...], limit)
    chunks = block // LANES
    wide_chunks = col_blocks * chunks
    parts[...] = jnp.zeros_like(parts)
    for pair in range(0, row_blocks, 2):
        for col in range(col_blocks):
            sums = [jnp.zeros((SUB, LANES), F32) for _ in range(2)]
            for chunk in range(chunks):
                k = col * chunks + chunk
                wide = grad[pair * SUB : (pair + 2) * SUB, k * LANES : (k + 1) * LANES].astype(F32)
                for side in range(2):
                    clipped = clip * wide[side * SUB : (side + 1) * SUB]
                    square = clipped * clipped
                    place = pl.ds((pair + side) * SUB * wide_chunks + k, SUB, stride=wide_chunks)
                    new = MOMENT_DECAY * second[place, :] + (1.0 - MOMENT_DECAY) * square
                    below = new * lax.rsqrt(new) + ADAM_EPS
                    sums[side] += square / (below * below)
            for side in range(2):
                b = (pair + side) * col_blocks + col
                parts[b : b + 1, :] = jnp.sum(sums[side], axis=0, keepdims=True)
    sums = lax.dot_general(
        jnp.ones((SUB, LANES), F32),
        parts[...],
        (((1,), (1,)), ((), ())),
        precision=lax.Precision.HIGHEST,
        preferred_element_type=F32,
    )
    lane = lax.broadcasted_iota(jnp.int32, (ROWS, LANES), 1)
    tile = jnp.where(lane == row_blocks * col_blocks, norm[:ROWS], sums[:ROWS])
    tail[...] = jnp.broadcast_to(spread(tile)[None], tail.shape)


def finish_kernel(limit, dp, block, wide_chunks, arrived, sq_a, sq_b, left, right, grad, second, left_new, right_new, moment):
    clip = clip_of(sq_a[...] + sq_b[...], limit)
    weight = (1.0 - STAT_DECAY) * clip[:, :1] * clip[:, :1] / block
    row = lax.broadcasted_iota(jnp.int32, (block, block), 0)
    col = lax.broadcasted_iota(jnp.int32, (block, block), 1)
    per = block // dp
    order = (row == (col % per) * dp + col // per).astype(BF16)
    g = arrived_block(block, arrived)
    right_new[...] = STAT_DECAY * right[...] + weight * dot(g, g, 0, 0)
    g = dot(order, g).astype(BF16)
    left_new[...] = STAT_DECAY * left[...] + weight * dot(g, g, 1, 1)
    for pair in range(0, grad.shape[0] // SUB, 2):
        for k in range(wide_chunks):
            wide = grad[pair * SUB : (pair + 2) * SUB, k * LANES : (k + 1) * LANES].astype(F32)
            for side in range(2):
                clipped = clip * wide[side * SUB : (side + 1) * SUB]
                place = pl.ds((pair + side) * SUB * wide_chunks + k, SUB, stride=wide_chunks)
                moment[place, :] = MOMENT_DECAY * second[place, :] + (1.0 - MOMENT_DECAY) * clipped * clipped


def place_kernel(row_blocks, col_blocks, block, owners, owner_lanes, returned, update, held, sems):
    blocks = row_blocks * col_blocks
    tiles = jnp.sum(returned[:, :, FOLDS * block :].astype(F32), axis=1)
    adam_sq = jnp.sum(tiles, axis=0, keepdims=True)[:, :blocks]
    slot = lax.broadcasted_iota(jnp.int32, (tiles.shape[0], blocks), 0)
    norms = jnp.where(owner_lanes[...] == slot, tiles[:, blocks : blocks + 1], 0.0)
    norm_sq = jnp.sum(norms, axis=0, keepdims=True)
    ratio = jnp.sqrt(adam_sq) / jnp.sqrt(norm_sq + NORM_EPS)
    copies = []
    for pair in range(row_blocks // 2):
        for col in range(col_blocks):
            rows = []
            for side in range(2):
                b = (2 * pair + side) * col_blocks + col
                rows.append(ratio[:, b : b + 1] * unfold(returned[pl.ds(owners[b], 1)], block)[0])
            here = slice(pair * 2 * SUB, (pair + 1) * 2 * SUB)
            held[here, col * block : (col + 1) * block] = jnp.concatenate(rows, axis=0).astype(BF16)
        span = pl.ds(pair * 2 * SUB, 2 * SUB)
        copies.append(pltpu.make_async_copy(held.at[span], update.at[span], sems.at[pair]))
        copies[-1].start()
    for copy in copies:
        copy.wait()


def on_device(gradient, second_moment, left_stat, right_stat, left_root, right_root, owner_table):
    dp = lax.axis_size("dp")
    experts = lax.axis_size("expert")
    _, local_rows, _, width = gradient.shape
    block = left_stat.shape[-1]
    row_blocks = local_rows // SUB
    col_blocks = width // block
    limit = math.sqrt(experts * local_rows * dp * width)
    grid = (row_blocks, col_blocks, block)
    grad = gradient.reshape(local_rows, width)
    second = second_moment.reshape(local_rows * width // LANES, LANES)
    owners = owner_table[0]
    packed = jax.ShapeDtypeStruct((dp, ROWS, FOLDS * block + LANES), BF16)
    square = functools.partial(jax.ShapeDtypeStruct, (block, block))
    line = jax.ShapeDtypeStruct((1, LANES), F32)
    cube = 2 * block**3
    area = block * block

    def exchange(x):
        return lax.all_to_all(x, "dp", split_axis=0, concat_axis=0, tiled=True)

    tail = pl.BlockSpec((dp, ROWS, LANES), lambda _: (0, 0, FOLDS * block // LANES))
    pairs = row_blocks // 2
    outgoing = call(
        functools.partial(pack_kernel, *grid), packed, [hbm(), hbm()], hbm(), "pack", moved=4 * area,
        scratch_shapes=[
            pltpu.SMEM(owner_table.shape, jnp.int32),
            pltpu.VMEM(grad.shape, BF16),
            pltpu.VMEM(packed.shape, BF16),
            pltpu.SemaphoreType.DMA((pairs + 1,)),
            pltpu.SemaphoreType.DMA((2,)),
        ],
        limit=PACK_LIMIT,
    )(owner_table, grad)
    arrived = exchange(outgoing)
    pair_of = jax.ShapeDtypeStruct((2, block, block), BF16)
    l_parts, r_parts = call(
        functools.partial(roots_kernel, dp), (pair_of,) * 2, [vmem()] * 2, (vmem(),) * 2, "roots",
        flops=4 * cube, moved=16 * area,
    )(left_root[0, 0], right_root[0, 0])
    sq_a = call(sum_kernel, line, [tail], vmem(), "norm", moved=area, grid=(1,))(arrived)
    sq_b = lax.ppermute(sq_a, "expert", [(j, j ^ 1) for j in range(experts)])
    half = call(
        functools.partial(left_kernel, block), square(F32), [vmem()] * 2, vmem(), "left",
        flops=2 * cube, moved=12 * area,
    )(l_parts, arrived)
    sq_a = sq_a + sq_b
    sq_b = lax.ppermute(sq_a, "expert", [(j, j ^ 3) for j in range(experts)])
    ready, norm = call(
        right_kernel, (packed, jax.ShapeDtypeStruct((SUB, LANES), F32)), [vmem()] * 2, (vmem(),) * 2, "right",
        flops=3 * cube, moved=10 * area,
    )(half, r_parts)
    ready = call(
        functools.partial(adam_kernel, limit, *grid), packed,
        [vmem()] * 5 + [pl.BlockSpec(memory_space=pl.ANY)], tail, "adam",
        moved=8 * area,
        scratch_shapes=[pltpu.VMEM((LANES, LANES), F32)],
        input_output_aliases={5: 0},
        grid=(1,),
    )(grad, second, sq_a, sq_b, norm, ready)
    returned = exchange(ready)
    left_new, right_new, moment = call(
        functools.partial(finish_kernel, limit, dp, block, width // LANES),
        (square(F32), square(F32), jax.ShapeDtypeStruct(second.shape, F32)),
        [vmem()] * 7, (vmem(),) * 3, "finish",
        flops=3 * cube, moved=28 * area,
    )(arrived, sq_a, sq_b, left_stat[0, 0], right_stat[0, 0], grad, second)
    update = call(
        functools.partial(place_kernel, *grid),
        jax.ShapeDtypeStruct((local_rows, width), BF16),
        [smem(), vmem(), vmem()], hbm(), "place",
        moved=4 * area,
        scratch_shapes=[pltpu.VMEM(grad.shape, BF16), pltpu.SemaphoreType.DMA((pairs,))],
    )(owners, owner_table, returned)
    return (
        update.reshape(gradient.shape),
        moment.reshape(second_moment.shape),
        left_new[None, None],
        right_new[None, None],
    )


def solution(mesh):
    rows = P("expert", None, "dp", None)
    slots = P("expert", "dp", None, None)
    return jax.shard_map(
        on_device,
        mesh=mesh,
        in_specs=(rows, rows, slots, slots, slots, slots, P("expert", None)),
        out_specs=(rows, rows, slots, slots),
        check_vma=False,
    )
```

time: 77.2 us -> 70.9 us (0.918)
  waiting for transfers between devices: 33.9 us -> 27.3 us
  Pallas kernels: 12.1 us -> 13.6 us
  local copies, waits for them, and re-layouts: 5.94 us -> 4.65 us
    all_to_all x2, waiting for transfers between devices: 33.9 us -> 27 us  [exchange(): return lax.all_to_all(x, 'dp', split_axis=0, concat_axis=0, tiled=True)]
    unnamed x32 -> x18, local copies, waits for them, and re-layouts: 5.94 us -> 4.65 us
    pallas_call x6, Pallas kernels: 8.57 us -> 9.77 us  [the longest x1 3.55 us: on_device(): call(functools.partial(finish_kernel, limit, dp, block, width // LANES),...]
  transfers between devices with their start and end apart: 4 -> 4, of which waited for: 2 -> 3; matrix products, arithmetic and copies ran while one was open for 0% -> 0% of each run, Pallas kernels for 8% -> 11%
where the time goes in v2:
time: 70.9 us; the launch traced here: 70.5 us
  waiting for transfers between devices  27.3 us (39%)
  starting transfers between devices  24.2 us (34%)
  Pallas kernels  13.6 us (19%)
  local copies, waits for them, and re-layouts  4.65 us (7%)
  between operations  0.72 us (1%)
    all_to_all x2, waiting for transfers between devices, exchange(): return lax.all_to_all(x, 'dp', split_axis=0, concat_axis=0, tiled=True)  27 us
    all_to_all x2, starting transfers between devices, exchange(): return lax.all_to_all(x, 'dp', split_axis=0, concat_axis=0, tiled=True)  20.5 us
    unnamed x18, local copies, waits for them, and re-layouts  4.65 us
    pallas_call x1, Pallas kernels, on_device(): call(functools.partial(finish_kernel, limit, dp, block, width // LANES),...  3.55 us
    ppermute x1, starting transfers between devices, on_device(): sq_b = lax.ppermute(sq_a, 'expert', [(j, j ^ 3) for j in range(experts)])  2.48 us
    pallas_call x1, Pallas kernels, on_device(): call(functools.partial(pack_kernel, *grid), packed, [hbm(), hbm()], hbm()...  2.1 us
    pallas_call x1, Pallas kernels, on_device(): call(right_kernel, (packed, jax.ShapeDtypeStruct((SUB, LANES), F32)), [vm...  2.04 us
    pallas_call x1, Pallas kernels, on_device(): call(functools.partial(place_kernel, *grid), jax.ShapeDtypeStruct((local_...  1.76 us
  transfers between devices with their start and end apart: 4, of which 3 were waited for; matrix products, arithmetic and copies ran while one was open for 0% of the time, Pallas kernels for 11%

profile of v2, /device:TPU:1, one launch (start us, length us, event | category | flops | bytes accessed | tf_op | source)
XLA Modules:
  0.0 70.5 jit_solution(5272946688397676998)
XLA Ops:
  0.6 2.1 %pack.1 = bf16[64,2,2176]{2,1,0:T(2,128)(2,1)} custom-call(s32[1,64]{1,0:T(1,128)} %owner_lanes.1, bf16[64,4096]{1,0:T(8,128)(2,1)} %bitcast.11), custom_call_target="tpu_custom_call" | custom-call | bytes 1048576 | tf_op jit(solution)/shard_map/pack/pallas_call | solution.py:242
  2.7 0.0 copy-start.5
  2.7 13.3 %all-to-all-start = ((bf16[64,2,2176]{2,1,0:T(2,128)(2,1)}), bf16[64,2,2176]{2,1,0:T(2,128)(2,1)S(1)}, u32[]{:S(2)}, u32[]{:S(2)}) async-start(bf16[64,2,2176]{2,1,0:T(2,128)(2,1)} %pack.1), calls=%async_computation | async-start | bytes 1114112 | tf_op jit(solution)/shard_map/all_to_all | solution.py:238
  16.1 0.0 copy-done.5
  16.1 0.0 copy-start.6
  16.1 1.2 %copy-done.6 = f32[1,1,512,512]{3,2,1,0:T(8,128)S(1)} copy-done((f32[1,1,512,512]{3,2,1,0:T(8,128)S(1)}, f32[1,1,512,512]{3,2,1,0:T(8,128)}, u32[]{:S(2)}) %copy-start.6) | copy-done | bytes 1048600
  17.3 1.5 %roots.1 = (bf16[2,512,512]{2,1,0:T(8,128)(2,1)S(1)}, bf16[2,512,512]{2,1,0:T(8,128)(2,1)S(1)}) custom-call(f32[512,512]{1,0:T(8,128)S(1)} %bitcast.19, f32[512,512]{1,0:T(8,128)S(1)} %bitcast.20), custom_call_target="tpu_custom_call" | custom-call | flops 1073741824 | bytes 4194304 | tf_op jit(solution)/shard_map/roots/pallas_call | solution.py:255
  18.8 0.0 copy-start.7
  18.8 1.0 %copy-done.7 = bf16[2,512,512]{2,1,0:T(8,128)(2,1)} copy-done((bf16[2,512,512]{2,1,0:T(8,128)(2,1)}, bf16[2,512,512]{2,1,0:T(8,128)(2,1)S(1)}, u32[]{:S(2)}) %copy-start.7) | copy-done | bytes 1048600
  19.8 14.7 %all-to-all-done.tiles.arrived = bf16[64,2,2176]{2,1,0:T(2,128)(2,1)S(1)} async-done(((bf16[64,2,2176]{2,1,0:T(2,128)(2,1)}), bf16[64,2,2176]{2,1,0:T(2,128)(2,1)S(1)}, u32[]{:S(2)}, u32[]{:S(2)}) %all-to-all-start) | async-done | bytes 557088 | tf_op jit(solution)/shard_map/all_to_all | solution.py:238
  34.4 0.1 norm.1
  34.5 1.3 %collective-permute-start = (f32[1,128]{1,0:T(1,128)S(1)}, f32[1,128]{1,0:T(1,128)S(1)}, u32[]{:S(2)}, u32[]{:S(2)}) collective-permute-start(f32[1,128]{1,0:T(1,128)S(1)} %norm.1), channel_id=1, source_target_pairs={{0,1},{1,0},{2,3},{3,2},{4,5},{5,4},{6,7},{7,6},{8,9},{9,8},{10,11... | collective-permute-start | bytes 1544 | tf_op jit(solution)/shard_map/ppermute | solution.py:260
  35.8 0.0 copy-start.8
  35.8 0.9 %left.1.half = f32[512,512]{1,0:T(8,128)S(1)} custom-call(bf16[2,512,512]{2,1,0:T(8,128)(2,1)S(1)} %get-tuple-element.11.l_parts, bf16[64,2,2176]{2,1,0:T(2,128)(2,1)S(1)} %all-to-all-done.tiles.arrived), custom_call_target="tpu_custom_call" | custom-call | flops 536870912 | bytes 3145728 | tf_op jit(solution)/shard_map/left/pallas_call | solution.py:261
  36.7 0.3 collective-permute-done
  37.0 2.5 %collective-permute-start.1 = (f32[1,128]{1,0:T(1,128)S(1)}, f32[1,128]{1,0:T(1,128)S(1)}, u32[]{:S(2)}, u32[]{:S(2)}) collective-permute-start(f32[1,128]{1,0:T(1,128)S(1)} %add.3.sq_a), channel_id=1, source_target_pairs={{0,3},{1,2},{2,1},{3,0},{4,7},{5,6},{6,5},{7,4},{8,11},{9,10},{10,... | collective-permute-start | bytes 1544 | tf_op jit(solution)/shard_map/ppermute | solution.py:266
  39.5 0.0 copy-done.8
  39.5 0.0 copy-start.1
  39.5 2.0 %right.1 = (bf16[64,2,2176]{2,1,0:T(2,128)(2,1)}, f32[8,128]{1,0:T(8,128)S(1)}) custom-call(f32[512,512]{1,0:T(8,128)S(1)} %left.1.half, bf16[2,512,512]{2,1,0:T(8,128)(2,1)S(1)} %copy-done.8), custom_call_target="tpu_custom_call" | custom-call | flops 805306368 | bytes 2621440 | tf_op jit(solution)/shard_map/right/pallas_call | solution.py:267
  41.5 0.0 collective-permute-done.1.sq_b
  41.5 0.0 copy-done
  41.5 0.0 copy-done.1
  41.6 1.6 %adam.1 = bf16[64,2,2176]{2,1,0:T(2,128)(2,1)} custom-call(bf16[64,4096]{1,0:T(8,128)(2,1)S(1)} %bitcast.12, f32[2048,128]{1,0:T(8,128)S(1)} %bitcast.14, f32[1,128]{1,0:T(1,128)S(1)} %add.3.sq_a, f32[1,128]{1,0:T(1,128)S(1)} %collective-permute-done.1.sq_b, f32[8,128]{1,0:T(8,128)S(1)} %get-tuple-element.13.norm, ...), custom_call_target="tpu_custom_call", output_to_operand_aliasing={{}: (5, {})} | custom-call | bytes 2097152 | tf_op jit(solution)/shard_map/adam/pallas_call | solution.py:271
  43.2 7.2 %all-to-all-start.1 = ((bf16[64,2,2176]{2,1,0:T(2,128)(2,1)}), bf16[64,2,2176]{2,1,0:T(2,128)(2,1)S(1)}, u32[]{:S(2)}, u32[]{:S(2)}) async-start(bf16[64,2,2176]{2,1,0:T(2,128)(2,1)} %adam.1), calls=%async_computation.1 | async-start | bytes 1114112 | tf_op jit(solution)/shard_map/all_to_all | solution.py:238
  50.4 0.0 copy-start.2
  50.4 1.2 %copy-done.2 = f32[1,1,512,512]{3,2,1,0:T(8,128)S(1)} copy-done((f32[1,1,512,512]{3,2,1,0:T(8,128)S(1)}, f32[1,1,512,512]{3,2,1,0:T(8,128)}, u32[]{:S(2)}) %copy-start.2) | copy-done | bytes 1048600
  51.6 0.0 copy-start.3
  51.6 1.2 %copy-done.3 = f32[1,1,512,512]{3,2,1,0:T(8,128)S(1)} copy-done((f32[1,1,512,512]{3,2,1,0:T(8,128)S(1)}, f32[1,1,512,512]{3,2,1,0:T(8,128)}, u32[]{:S(2)}) %copy-start.3) | copy-done | bytes 1048600
  52.8 3.5 %finish.1 = (f32[512,512]{1,0:T(8,128)}, f32[512,512]{1,0:T(8,128)}, f32[2048,128]{1,0:T(8,128)}) custom-call(bf16[64,2,2176]{2,1,0:T(2,128)(2,1)S(1)} %all-to-all-done.tiles.arrived, f32[1,128]{1,0:T(1,128)S(1)} %add.3.sq_a, f32[1,128]{1,0:T(1,128)S(1)} %collective-permute-done.1.sq_b, f32[512,512]{1,0:T(8,128)S(1)} %bitcast.16, f32[512,512]{1,0:T(8,128)S(1)} %bitcast.17, ...), custom_call_target="tpu_custom_call" | custom-call | flops 805306368 | bytes 7340032 | tf_op jit(solution)/shard_map/finish/pallas_call | solution.py:280
  56.4 12.4 %all-to-all-done.1.returned = bf16[64,2,2176]{2,1,0:T(2,128)(2,1)S(1)} async-done(((bf16[64,2,2176]{2,1,0:T(2,128)(2,1)}), bf16[64,2,2176]{2,1,0:T(2,128)(2,1)S(1)}, u32[]{:S(2)}, u32[]{:S(2)}) %all-to-all-start.1) | async-done | bytes 557088 | tf_op jit(solution)/shard_map/all_to_all | solution.py:238
  68.8 0.0 copy-done.4
  68.8 1.8 %place.1 = bf16[64,4096]{1,0:T(8,128)(2,1)} custom-call(s32[64]{0:T(128)S(1)} %bitcast.18, s32[1,64]{1,0:T(1,128)S(1)} %copy-done.4, bf16[64,2,2176]{2,1,0:T(2,128)(2,1)S(1)} %all-to-all-done.1.returned), custom_call_target="tpu_custom_call" | custom-call | bytes 1048576 | tf_op jit(solution)/shard_map/place/pallas_call | solution.py:286
  (3 shorter events, 0.0 us)
Async XLA Ops:
  2.7 13.3 %copy-start.5 = (f32[1,1,512,512]{3,2,1,0:T(8,128)S(1)}, f32[1,1,512,512]{3,2,1,0:T(8,128)}, u32[]{:S(2)}) copy-start(f32[1,1,512,512]{3,2,1,0:T(8,128)} %param.11) | copy-start | bytes 3145732
  2.7 31.7 %all-to-all-start = ((bf16[64,2,2176]{2,1,0:T(2,128)(2,1)}), bf16[64,2,2176]{2,1,0:T(2,128)(2,1)S(1)}, u32[]{:S(2)}, u32[]{:S(2)}) async-start(bf16[64,2,2176]{2,1,0:T(2,128)(2,1)} %pack.1), calls=%async_computation | async-start | bytes 1114112 | tf_op jit(solution)/shard_map/all_to_all | solution.py:238
  16.1 1.2 %copy-start.6 = (f32[1,1,512,512]{3,2,1,0:T(8,128)S(1)}, f32[1,1,512,512]{3,2,1,0:T(8,128)}, u32[]{:S(2)}) copy-start(f32[1,1,512,512]{3,2,1,0:T(8,128)} %param.12) | copy-start | bytes 3145732
  18.8 1.0 %copy-start.7 = (bf16[2,512,512]{2,1,0:T(8,128)(2,1)}, bf16[2,512,512]{2,1,0:T(8,128)(2,1)S(1)}, u32[]{:S(2)}) copy-start(bf16[2,512,512]{2,1,0:T(8,128)(2,1)S(1)} %get-tuple-element.12.r_parts) | copy-start | bytes 3145732
  34.5 2.5 %collective-permute-start = (f32[1,128]{1,0:T(1,128)S(1)}, f32[1,128]{1,0:T(1,128)S(1)}, u32[]{:S(2)}, u32[]{:S(2)}) collective-permute-start(f32[1,128]{1,0:T(1,128)S(1)} %norm.1), channel_id=1, source_target_pairs={{0,1},{1,0},{2,3},{3,2},{4,5},{5,4},{6,7},{7,6},{8,9},{9,8},{10,11... | collective-permute-start | bytes 1544 | tf_op jit(solution)/shard_map/ppermute | solution.py:260
  35.8 3.7 %copy-start.8 = (bf16[2,512,512]{2,1,0:T(8,128)(2,1)S(1)}, bf16[2,512,512]{2,1,0:T(8,128)(2,1)}, u32[]{:S(2)}) copy-start(bf16[2,512,512]{2,1,0:T(8,128)(2,1)} %copy-done.7) | copy-start | bytes 3145732
  37.0 4.5 %collective-permute-start.1 = (f32[1,128]{1,0:T(1,128)S(1)}, f32[1,128]{1,0:T(1,128)S(1)}, u32[]{:S(2)}, u32[]{:S(2)}) collective-permute-start(f32[1,128]{1,0:T(1,128)S(1)} %add.3.sq_a), channel_id=1, source_target_pairs={{0,3},{1,2},{2,1},{3,0},{4,7},{5,6},{6,5},{7,4},{8,11},{9,10},{10,... | collective-permute-start | bytes 1544 | tf_op jit(solution)/shard_map/ppermute | solution.py:266
  39.5 2.1 %copy-start = (bf16[1,64,1,4096]{3,1,2,0:T(8,128)(2,1)S(1)}, bf16[1,64,1,4096]{3,1,2,0:T(8,128)(2,1)}, u32[]{:S(2)}) copy-start(bf16[1,64,1,4096]{3,1,2,0:T(8,128)(2,1)} %param.7) | copy-start | bytes 1572868
  39.5 2.1 %copy-start.1 = (f32[1,64,1,4096]{3,2,1,0:T(1,128)S(1)}, f32[1,64,1,4096]{3,2,1,0:T(1,128)}, u32[]{:S(2)}) copy-start(f32[1,64,1,4096]{3,2,1,0:T(1,128)} %param.8) | copy-start | bytes 3145732
  43.2 25.6 %all-to-all-start.1 = ((bf16[64,2,2176]{2,1,0:T(2,128)(2,1)}), bf16[64,2,2176]{2,1,0:T(2,128)(2,1)S(1)}, u32[]{:S(2)}, u32[]{:S(2)}) async-start(bf16[64,2,2176]{2,1,0:T(2,128)(2,1)} %adam.1), calls=%async_computation.1 | async-start | bytes 1114112 | tf_op jit(solution)/shard_map/all_to_all | solution.py:238
  50.4 1.2 %copy-start.2 = (f32[1,1,512,512]{3,2,1,0:T(8,128)S(1)}, f32[1,1,512,512]{3,2,1,0:T(8,128)}, u32[]{:S(2)}) copy-start(f32[1,1,512,512]{3,2,1,0:T(8,128)} %param.9) | copy-start | bytes 3145732
  51.6 1.2 %copy-start.3 = (f32[1,1,512,512]{3,2,1,0:T(8,128)S(1)}, f32[1,1,512,512]{3,2,1,0:T(8,128)}, u32[]{:S(2)}) copy-start(f32[1,1,512,512]{3,2,1,0:T(8,128)} %param.10) | copy-start | bytes 3145732
  56.4 12.4 %copy-start.4 = (s32[1,64]{1,0:T(1,128)S(1)}, s32[1,64]{1,0:T(1,128)}, u32[]{:S(2)}) copy-start(s32[1,64]{1,0:T(1,128)} %owner_lanes.1) | copy-start | bytes 772

commit v3 on v2

--- a/solution.py
+++ b/solution.py
@@ -93,7 +93,11 @@
                 piece = wide[side * SUB : (side + 1) * SUB]
                 total += piece * piece
                 slot = owners[0, (2 * pair + side) * col_blocks + col]
-                ready[slot, :, : FOLDS * block] = fold(piece[None])[0]
+                at = pair * rows + side * SUB
+                for i in range(FOLDS):
+                    ready[slot, :, i * block : (i + 1) * block] = held[
+                        at + i * ROWS : at + (i + 1) * ROWS, col * block : (col + 1) * block
+                    ]
                 pltpu.make_async_copy(
                     ready.at[slot, :, : FOLDS * block], out.at[slot, :, : FOLDS * block], out_sems.at[0]
                 ).start()
@@ -139,8 +143,8 @@
     out[:, :, : FOLDS * block] = fold(full.reshape(out.shape[0], SUB, block))
 
 
-def adam_kernel(limit, row_blocks, col_blocks, block, grad, second, sq_a, sq_b, norm, _, tail, parts):
-    clip = clip_of(sq_a[...] + sq_b[...], limit)
+def adam_kernel(limit, row_blocks, col_blocks, block, grad, second, sq_0, sq_1, sq_2, sq_3, norm, _, tail, parts):
+    clip = clip_of((sq_0[...] + sq_1[...]) + (sq_2[...] + sq_3[...]), limit)
     chunks = block // LANES
     wide_chunks = col_blocks * chunks
     parts[...] = jnp.zeros_like(parts)
@@ -172,8 +176,8 @@
     tail[...] = jnp.broadcast_to(spread(tile)[None], tail.shape)
 
 
-def finish_kernel(limit, dp, block, wide_chunks, arrived, sq_a, sq_b, left, right, grad, second, left_new, right_new, moment):
-    clip = clip_of(sq_a[...] + sq_b[...], limit)
+def finish_kernel(limit, dp, block, wide_chunks, arrived, sq_0, sq_1, sq_2, sq_3, left, right, grad, second, left_new, right_new, moment):
+    clip = clip_of((sq_0[...] + sq_1[...]) + (sq_2[...] + sq_3[...]), limit)
     weight = (1.0 - STAT_DECAY) * clip[:, :1] * clip[:, :1] / block
     row = lax.broadcasted_iota(jnp.int32, (block, block), 0)
     col = lax.broadcasted_iota(jnp.int32, (block, block), 1)
@@ -192,7 +196,9 @@
                 moment[place, :] = MOMENT_DECAY * second[place, :] + (1.0 - MOMENT_DECAY) * clipped * clipped
 
 
-def place_kernel(row_blocks, col_blocks, block, owners, owner_lanes, returned, update, held, sems):
+def place_kernel(row_blocks, col_blocks, block, table, owner_lanes, returned, update, owners, held, sems):
+    placing = pltpu.make_async_copy(table, owners, sems.at[row_blocks // 2])
+    placing.start()
     blocks = row_blocks * col_blocks
     tiles = jnp.sum(returned[:, :, FOLDS * block :].astype(F32), axis=1)
     adam_sq = jnp.sum(tiles, axis=0, keepdims=True)[:, :blocks]
@@ -200,13 +206,14 @@
     norms = jnp.where(owner_lanes[...] == slot, tiles[:, blocks : blocks + 1], 0.0)
     norm_sq = jnp.sum(norms, axis=0, keepdims=True)
     ratio = jnp.sqrt(adam_sq) / jnp.sqrt(norm_sq + NORM_EPS)
+    placing.wait()
     copies = []
     for pair in range(row_blocks // 2):
         for col in range(col_blocks):
             rows = []
             for side in range(2):
                 b = (2 * pair + side) * col_blocks + col
-                rows.append(ratio[:, b : b + 1] * unfold(returned[pl.ds(owners[b], 1)], block)[0])
+                rows.append(ratio[:, b : b + 1] * unfold(returned[pl.ds(owners[0, b], 1)], block)[0])
             here = slice(pair * 2 * SUB, (pair + 1) * 2 * SUB)
             held[here, col * block : (col + 1) * block] = jnp.concatenate(rows, axis=0).astype(BF16)
         span = pl.ds(pair * 2 * SUB, 2 * SUB)
@@ -239,6 +246,10 @@
 
     tail = pl.BlockSpec((dp, ROWS, LANES), lambda _: (0, 0, FOLDS * block // LANES))
     pairs = row_blocks // 2
+    def swap(x, step):
+        pairs = [(i * experts + j, (i ^ 1) * experts + (j ^ step)) for i in range(dp) for j in range(experts)]
+        return lax.ppermute(x, ("dp", "expert"), pairs)
+
     outgoing = call(
         functools.partial(pack_kernel, *grid), packed, [hbm(), hbm()], hbm(), "pack", moved=4 * area,
         scratch_shapes=[
@@ -257,39 +268,41 @@
         flops=4 * cube, moved=16 * area,
     )(left_root[0, 0], right_root[0, 0])
     sq_a = call(sum_kernel, line, [tail], vmem(), "norm", moved=area, grid=(1,))(arrived)
-    sq_b = lax.ppermute(sq_a, "expert", [(j, j ^ 1) for j in range(experts)])
+    sqs = [sq_a] + [swap(sq_a, step) for step in range(1, experts)]
     half = call(
         functools.partial(left_kernel, block), square(F32), [vmem()] * 2, vmem(), "left",
         flops=2 * cube, moved=12 * area,
     )(l_parts, arrived)
-    sq_a = sq_a + sq_b
-    sq_b = lax.ppermute(sq_a, "expert", [(j, j ^ 3) for j in range(experts)])
     ready, norm = call(
         right_kernel, (packed, jax.ShapeDtypeStruct((SUB, LANES), F32)), [vmem()] * 2, (vmem(),) * 2, "right",
         flops=3 * cube, moved=10 * area,
     )(half, r_parts)
     ready = call(
         functools.partial(adam_kernel, limit, *grid), packed,
-        [vmem()] * 5 + [pl.BlockSpec(memory_space=pl.ANY)], tail, "adam",
+        [vmem()] * 7 + [pl.BlockSpec(memory_space=pl.ANY)], tail, "adam",
         moved=8 * area,
         scratch_shapes=[pltpu.VMEM((LANES, LANES), F32)],
-        input_output_aliases={5: 0},
+        input_output_aliases={7: 0},
         grid=(1,),
-    )(grad, second, sq_a, sq_b, norm, ready)
+    )(grad, second, *sqs, norm, ready)
     returned = exchange(ready)
     left_new, right_new, moment = call(
         functools.partial(finish_kernel, limit, dp, block, width // LANES),
         (square(F32), square(F32), jax.ShapeDtypeStruct(second.shape, F32)),
-        [vmem()] * 7, (vmem(),) * 3, "finish",
+        [vmem()] * 9, (vmem(),) * 3, "finish",
         flops=3 * cube, moved=28 * area,
-    )(arrived, sq_a, sq_b, left_stat[0, 0], right_stat[0, 0], grad, second)
+    )(arrived, *sqs, left_stat[0, 0], right_stat[0, 0], grad, second)
     update = call(
         functools.partial(place_kernel, *grid),
         jax.ShapeDtypeStruct((local_rows, width), BF16),
-        [smem(), vmem(), vmem()], hbm(), "place",
+        [hbm(), vmem(), vmem()], hbm(), "place",
         moved=4 * area,
-        scratch_shapes=[pltpu.VMEM(grad.shape, BF16), pltpu.SemaphoreType.DMA((pairs,))],
-    )(owners, owner_table, returned)
+        scratch_shapes=[
+            pltpu.SMEM(owner_table.shape, jnp.int32),
+            pltpu.VMEM(grad.shape, BF16),
+            pltpu.SemaphoreType.DMA((pairs + 1,)),
+        ],
+    )(owner_table, owner_table, returned)
     return (
         update.reshape(gradient.shape),
         moment.reshape(second_moment.shape),

time: 70.9 us -> 69.3 us (0.977)
  starting transfers between devices: 24.2 us -> 22.7 us
    all_to_all x2, starting transfers between devices: 20.5 us -> 18.7 us  [exchange(): return lax.all_to_all(x, 'dp', split_axis=0, concat_axis=0, tiled=True)]
    ppermute x2 -> x3, starting transfers between devices: 3.77 us -> 3.94 us  [swap(): return lax.ppermute(x, ('dp', 'expert'), pairs)]
  transfers between devices with their start and end apart: 4 -> 5, of which waited for: 3 -> 3; matrix products, arithmetic and copies ran while one was open for 0% -> 0% of each run, Pallas kernels for 11% -> 12%
where the time goes in v3:
time: 69.3 us; the launch traced here: 68.9 us
  waiting for transfers between devices  27.2 us (39%)
  starting transfers between devices  22.7 us (33%)
  Pallas kernels  13.3 us (19%)
  local copies, waits for them, and re-layouts  4.97 us (7%)
  between operations  0.72 us (1%)
    all_to_all x2, waiting for transfers between devices, exchange(): return lax.all_to_all(x, 'dp', split_axis=0, concat_axis=0, tiled=True)  27.1 us
    all_to_all x2, starting transfers between devices, exchange(): return lax.all_to_all(x, 'dp', split_axis=0, concat_axis=0, tiled=True)  18.7 us
    unnamed x18, local copies, waits for them, and re-layouts  4.97 us
    ppermute x3, starting transfers between devices, swap(): return lax.ppermute(x, ('dp', 'expert'), pairs)  3.94 us
    pallas_call x1, Pallas kernels, on_device(): call(functools.partial(finish_kernel, limit, dp, block, width // LANES),...  3.54 us
    pallas_call x1, Pallas kernels, on_device(): call(right_kernel, (packed, jax.ShapeDtypeStruct((SUB, LANES), F32)), [vm...  2.03 us
    pallas_call x1, Pallas kernels, on_device(): call(functools.partial(pack_kernel, *grid), packed, [hbm(), hbm()], hbm()...  2 us
    pallas_call x1, Pallas kernels, on_device(): call(functools.partial(adam_kernel, limit, *grid), packed, [vmem()] * 7 +...  1.65 us
  transfers between devices with their start and end apart: 5, of which 3 were waited for; matrix products, arithmetic and copies ran while one was open for 0% of the time, Pallas kernels for 12%

profile of v3, /device:TPU:1, one launch (start us, length us, event | category | flops | bytes accessed | tf_op | source)
XLA Modules:
  0.0 68.9 jit_solution(7563202689780762958)
XLA Ops:
  0.6 2.0 %pack.1 = bf16[64,2,2176]{2,1,0:T(2,128)(2,1)} custom-call(s32[1,64]{1,0:T(1,128)} %owner_lanes.1, bf16[64,4096]{1,0:T(8,128)(2,1)} %bitcast.10), custom_call_target="tpu_custom_call" | custom-call | bytes 1048576 | tf_op jit(solution)/shard_map/pack/pallas_call | solution.py:253
  2.6 0.0 copy-start.5
  2.7 13.3 %all-to-all-start = ((bf16[64,2,2176]{2,1,0:T(2,128)(2,1)}), bf16[64,2,2176]{2,1,0:T(2,128)(2,1)S(1)}, u32[]{:S(2)}, u32[]{:S(2)}) async-start(bf16[64,2,2176]{2,1,0:T(2,128)(2,1)} %pack.1), calls=%async_computation | async-start | bytes 1114112 | tf_op jit(solution)/shard_map/all_to_all | solution.py:245
  16.0 0.0 copy-done.5
  16.0 0.0 copy-start.6
  16.0 1.2 %copy-done.6 = f32[1,1,512,512]{3,2,1,0:T(8,128)S(1)} copy-done((f32[1,1,512,512]{3,2,1,0:T(8,128)S(1)}, f32[1,1,512,512]{3,2,1,0:T(8,128)}, u32[]{:S(2)}) %copy-start.6) | copy-done | bytes 1048600
  17.2 1.5 %roots.1 = (bf16[2,512,512]{2,1,0:T(8,128)(2,1)S(1)}, bf16[2,512,512]{2,1,0:T(8,128)(2,1)S(1)}) custom-call(f32[512,512]{1,0:T(8,128)S(1)} %bitcast.17, f32[512,512]{1,0:T(8,128)S(1)} %bitcast.18), custom_call_target="tpu_custom_call" | custom-call | flops 1073741824 | bytes 4194304 | tf_op jit(solution)/shard_map/roots/pallas_call | solution.py:266
  18.7 0.0 copy-start.7
  18.7 1.0 %copy-done.7 = bf16[2,512,512]{2,1,0:T(8,128)(2,1)} copy-done((bf16[2,512,512]{2,1,0:T(8,128)(2,1)}, bf16[2,512,512]{2,1,0:T(8,128)(2,1)S(1)}, u32[]{:S(2)}) %copy-start.7) | copy-done | bytes 1048600
  19.7 14.7 %all-to-all-done.tiles.arrived = bf16[64,2,2176]{2,1,0:T(2,128)(2,1)S(1)} async-done(((bf16[64,2,2176]{2,1,0:T(2,128)(2,1)}), bf16[64,2,2176]{2,1,0:T(2,128)(2,1)S(1)}, u32[]{:S(2)}, u32[]{:S(2)}) %all-to-all-start) | async-done | bytes 557088 | tf_op jit(solution)/shard_map/all_to_all | solution.py:245
  34.3 0.1 norm.1.sq_0
  34.4 2.9 %collective-permute-start.2 = (f32[1,128]{1,0:T(1,128)S(1)}, f32[1,128]{1,0:T(1,128)S(1)}, u32[]{:S(2)}, u32[]{:S(2)}) collective-permute-start(f32[1,128]{1,0:T(1,128)S(1)} %norm.1.sq_0), channel_id=1, source_target_pairs={{0,7},{1,6},{2,5},{3,4},{4,3},{5,2},{6,1},{7,0},{8,15},{9,14},{10,... | collective-permute-start | bytes 1544 | tf_op jit(solution)/shard_map/ppermute | solution.py:251
  37.3 0.5 collective-permute-start.1
  37.8 0.6 collective-permute-start
  38.4 0.0 copy-start.8
  38.4 0.9 %left.1.half = f32[512,512]{1,0:T(8,128)S(1)} custom-call(bf16[2,512,512]{2,1,0:T(8,128)(2,1)S(1)} %get-tuple-element.11.l_parts, bf16[64,2,2176]{2,1,0:T(2,128)(2,1)S(1)} %all-to-all-done.tiles.arrived), custom_call_target="tpu_custom_call" | custom-call | flops 536870912 | bytes 3145728 | tf_op jit(solution)/shard_map/left/pallas_call | solution.py:272
  39.3 0.3 copy-done.8
  39.6 2.0 %right.1 = (bf16[64,2,2176]{2,1,0:T(2,128)(2,1)}, f32[8,128]{1,0:T(8,128)S(1)}) custom-call(f32[512,512]{1,0:T(8,128)S(1)} %left.1.half, bf16[2,512,512]{2,1,0:T(8,128)(2,1)S(1)} %copy-done.8), custom_call_target="tpu_custom_call" | custom-call | flops 805306368 | bytes 2621440 | tf_op jit(solution)/shard_map/right/pallas_call | solution.py:276
  41.6 0.0 collective-permute-done.2.sq_3
  41.6 0.1 collective-permute-done.1.sq_2
  41.8 0.0 collective-permute-done.sq_1
  41.8 0.0 copy-done
  41.8 0.0 copy-done.1
  41.8 1.7 %adam.1 = bf16[64,2,2176]{2,1,0:T(2,128)(2,1)} custom-call(bf16[64,4096]{1,0:T(8,128)(2,1)S(1)} %bitcast.11, f32[2048,128]{1,0:T(8,128)S(1)} %bitcast.13, f32[1,128]{1,0:T(1,128)S(1)} %norm.1.sq_0, f32[1,128]{1,0:T(1,128)S(1)} %collective-permute-done.sq_1, f32[1,128]{1,0:T(1,128)S(1)} %collective-permute-done.1.sq_2, ...), custom_call_target="tpu_custom_call", output_to_operand_aliasing={{}: (7, {})} | custom-call | bytes 2097152 | tf_op jit(solution)/shard_map/adam/pallas_call | solution.py:280
  43.5 5.4 %all-to-all-start.1 = ((bf16[64,2,2176]{2,1,0:T(2,128)(2,1)}), bf16[64,2,2176]{2,1,0:T(2,128)(2,1)S(1)}, u32[]{:S(2)}, u32[]{:S(2)}) async-start(bf16[64,2,2176]{2,1,0:T(2,128)(2,1)} %adam.1), calls=%async_computation.1 | async-start | bytes 1114112 | tf_op jit(solution)/shard_map/all_to_all | solution.py:245
  48.9 0.0 copy-start.2
  48.9 1.2 %copy-done.2 = f32[1,1,512,512]{3,2,1,0:T(8,128)S(1)} copy-done((f32[1,1,512,512]{3,2,1,0:T(8,128)S(1)}, f32[1,1,512,512]{3,2,1,0:T(8,128)}, u32[]{:S(2)}) %copy-start.2) | copy-done | bytes 1048600
  50.1 1.2 %copy-done.3 = f32[1,1,512,512]{3,2,1,0:T(8,128)S(1)} copy-done((f32[1,1,512,512]{3,2,1,0:T(8,128)S(1)}, f32[1,1,512,512]{3,2,1,0:T(8,128)}, u32[]{:S(2)}) %copy-start.3) | copy-done | bytes 1048600
  51.3 3.5 %finish.1 = (f32[512,512]{1,0:T(8,128)}, f32[512,512]{1,0:T(8,128)}, f32[2048,128]{1,0:T(8,128)}) custom-call(bf16[64,2,2176]{2,1,0:T(2,128)(2,1)S(1)} %all-to-all-done.tiles.arrived, f32[1,128]{1,0:T(1,128)S(1)} %norm.1.sq_0, f32[1,128]{1,0:T(1,128)S(1)} %collective-permute-done.sq_1, f32[1,128]{1,0:T(1,128)S(1)} %collective-permute-done.1.sq_2, ...), custom_call_target="tpu_custom_call" | custom-call | flops 805306368 | bytes 7340032 | tf_op jit(solution)/shard_map/finish/pallas_call | solution.py:289
  54.9 12.4 %all-to-all-done.1.returned = bf16[64,2,2176]{2,1,0:T(2,128)(2,1)S(1)} async-done(((bf16[64,2,2176]{2,1,0:T(2,128)(2,1)}), bf16[64,2,2176]{2,1,0:T(2,128)(2,1)S(1)}, u32[]{:S(2)}, u32[]{:S(2)}) %all-to-all-start.1) | async-done | bytes 557088 | tf_op jit(solution)/shard_map/all_to_all | solution.py:245
  67.3 0.0 copy-done.4
  67.3 1.6 %place.1 = bf16[64,4096]{1,0:T(8,128)(2,1)} custom-call(s32[1,64]{1,0:T(1,128)S(1)} %copy-done.4, s32[1,64]{1,0:T(1,128)S(1)} %copy-done.4, bf16[64,2,2176]{2,1,0:T(2,128)(2,1)S(1)} %all-to-all-done.1.returned), custom_call_target="tpu_custom_call" | custom-call | bytes 1048576 | tf_op jit(solution)/shard_map/place/pallas_call | solution.py:295
  (4 shorter events, 0.0 us)
Async XLA Ops:
  2.6 13.3 %copy-start.5 = (f32[1,1,512,512]{3,2,1,0:T(8,128)S(1)}, f32[1,1,512,512]{3,2,1,0:T(8,128)}, u32[]{:S(2)}) copy-start(f32[1,1,512,512]{3,2,1,0:T(8,128)} %param.11) | copy-start | bytes 3145732
  2.7 31.7 %all-to-all-start = ((bf16[64,2,2176]{2,1,0:T(2,128)(2,1)}), bf16[64,2,2176]{2,1,0:T(2,128)(2,1)S(1)}, u32[]{:S(2)}, u32[]{:S(2)}) async-start(bf16[64,2,2176]{2,1,0:T(2,128)(2,1)} %pack.1), calls=%async_computation | async-start | bytes 1114112 | tf_op jit(solution)/shard_map/all_to_all | solution.py:245
  16.0 1.2 %copy-start.6 = (f32[1,1,512,512]{3,2,1,0:T(8,128)S(1)}, f32[1,1,512,512]{3,2,1,0:T(8,128)}, u32[]{:S(2)}) copy-start(f32[1,1,512,512]{3,2,1,0:T(8,128)} %param.12) | copy-start | bytes 3145732
  18.7 1.0 %copy-start.7 = (bf16[2,512,512]{2,1,0:T(8,128)(2,1)}, bf16[2,512,512]{2,1,0:T(8,128)(2,1)S(1)}, u32[]{:S(2)}) copy-start(bf16[2,512,512]{2,1,0:T(8,128)(2,1)S(1)} %get-tuple-element.12.r_parts) | copy-start | bytes 3145732
  34.4 7.2 %collective-permute-start.2 = (f32[1,128]{1,0:T(1,128)S(1)}, f32[1,128]{1,0:T(1,128)S(1)}, u32[]{:S(2)}, u32[]{:S(2)}) collective-permute-start(f32[1,128]{1,0:T(1,128)S(1)} %norm.1.sq_0), channel_id=1, source_target_pairs={{0,7},{1,6},{2,5},{3,4},{4,3},{5,2},{6,1},{7,0},{8,15},{9,14},{10,... | collective-permute-start | bytes 1544 | tf_op jit(solution)/shard_map/ppermute | solution.py:251
  37.3 4.5 %collective-permute-start.1 = (f32[1,128]{1,0:T(1,128)S(1)}, f32[1,128]{1,0:T(1,128)S(1)}, u32[]{:S(2)}, u32[]{:S(2)}) collective-permute-start(f32[1,128]{1,0:T(1,128)S(1)} %norm.1.sq_0), channel_id=1, source_target_pairs={{0,6},{1,7},{2,4},{3,5},{4,2},{5,3},{6,0},{7,1},{8,14},{9,15},{10,... | collective-permute-start | bytes 1544 | tf_op jit(solution)/shard_map/ppermute | solution.py:251
  37.8 4.0 %collective-permute-start = (f32[1,128]{1,0:T(1,128)S(1)}, f32[1,128]{1,0:T(1,128)S(1)}, u32[]{:S(2)}, u32[]{:S(2)}) collective-permute-start(f32[1,128]{1,0:T(1,128)S(1)} %norm.1.sq_0), channel_id=1, source_target_pairs={{0,5},{1,4},{2,7},{3,6},{4,1},{5,0},{6,3},{7,2},{8,13},{9,12},{10,... | collective-permute-start | bytes 1544 | tf_op jit(solution)/shard_map/ppermute | solution.py:251
  38.4 1.2 %copy-start.8 = (bf16[2,512,512]{2,1,0:T(8,128)(2,1)S(1)}, bf16[2,512,512]{2,1,0:T(8,128)(2,1)}, u32[]{:S(2)}) copy-start(bf16[2,512,512]{2,1,0:T(8,128)(2,1)} %copy-done.7) | copy-start | bytes 3145732
  39.6 2.2 %copy-start = (bf16[1,64,1,4096]{3,1,2,0:T(8,128)(2,1)S(1)}, bf16[1,64,1,4096]{3,1,2,0:T(8,128)(2,1)}, u32[]{:S(2)}) copy-start(bf16[1,64,1,4096]{3,1,2,0:T(8,128)(2,1)} %param.7) | copy-start | bytes 1572868
  39.6 2.2 %copy-start.1 = (f32[1,64,1,4096]{3,2,1,0:T(1,128)S(1)}, f32[1,64,1,4096]{3,2,1,0:T(1,128)}, u32[]{:S(2)}) copy-start(f32[1,64,1,4096]{3,2,1,0:T(1,128)} %param.8) | copy-start | bytes 3145732
  43.5 23.8 %all-to-all-start.1 = ((bf16[64,2,2176]{2,1,0:T(2,128)(2,1)}), bf16[64,2,2176]{2,1,0:T(2,128)(2,1)S(1)}, u32[]{:S(2)}, u32[]{:S(2)}) async-start(bf16[64,2,2176]{2,1,0:T(2,128)(2,1)} %adam.1), calls=%async_computation.1 | async-start | bytes 1114112 | tf_op jit(solution)/shard_map/all_to_all | solution.py:245
  48.9 1.2 %copy-start.2 = (f32[1,1,512,512]{3,2,1,0:T(8,128)S(1)}, f32[1,1,512,512]{3,2,1,0:T(8,128)}, u32[]{:S(2)}) copy-start(f32[1,1,512,512]{3,2,1,0:T(8,128)} %param.9) | copy-start | bytes 3145732
  50.1 1.2 %copy-start.3 = (f32[1,1,512,512]{3,2,1,0:T(8,128)S(1)}, f32[1,1,512,512]{3,2,1,0:T(8,128)}, u32[]{:S(2)}) copy-start(f32[1,1,512,512]{3,2,1,0:T(8,128)} %param.10) | copy-start | bytes 3145732
  51.3 15.9 %copy-start.4 = (s32[1,64]{1,0:T(1,128)S(1)}, s32[1,64]{1,0:T(1,128)}, u32[]{:S(2)}) copy-start(s32[1,64]{1,0:T(1,128)} %owner_lanes.1) | copy-start | bytes 772

commit v4 on v3

--- a/solution.py
+++ b/solution.py
@@ -67,7 +67,7 @@
 
 
 def unfold(x, block):
-    return jnp.concatenate([x[:, :, i * block : (i + 1) * block].astype(F32) for i in range(FOLDS)], axis=1)
+    return jnp.concatenate([x[:, :, i * block : (i + 1) * block] for i in range(FOLDS)], axis=1).astype(F32)
 
 
 def clip_of(grad_sq, limit):
@@ -140,10 +140,14 @@
     high, low = split2(half[...])
     full = dot(high, r_parts[0]) + dot(high, r_parts[1]) + dot(low, r_parts[0])
     norm[...] = jnp.broadcast_to(jnp.sum(full * full, keepdims=True), norm.shape)
-    out[:, :, : FOLDS * block] = fold(full.reshape(out.shape[0], SUB, block))
-
-
-def adam_kernel(limit, row_blocks, col_blocks, block, grad, second, sq_0, sq_1, sq_2, sq_3, norm, _, tail, parts):
+    whole = full.reshape(out.shape[0], SUB, block)
+    for i in range(FOLDS):
+        out[:, :, i * block : (i + 1) * block] = whole[:, i * ROWS : (i + 1) * ROWS].astype(BF16)
+
+
+def adam_kernel(limit, row_blocks, col_blocks, block, grad, second, sq_0, sq_1, sq_2, sq_3, norm, data, out, parts, tail, sems):
+    body = pltpu.make_async_copy(data, out.at[:, :, : FOLDS * block], sems.at[0])
+    body.start()
     clip = clip_of((sq_0[...] + sq_1[...]) + (sq_2[...] + sq_3[...]), limit)
     chunks = block // LANES
     wide_chunks = col_blocks * chunks
@@ -174,6 +178,10 @@
     lane = lax.broadcasted_iota(jnp.int32, (ROWS, LANES), 1)
     tile = jnp.where(lane == row_blocks * col_blocks, norm[:ROWS], sums[:ROWS])
     tail[...] = jnp.broadcast_to(spread(tile)[None], tail.shape)
+    end = pltpu.make_async_copy(tail, out.at[:, :, FOLDS * block :], sems.at[1])
+    end.start()
+    body.wait()
+    end.wait()
 
 
 def finish_kernel(limit, dp, block, wide_chunks, arrived, sq_0, sq_1, sq_2, sq_3, left, right, grad, second, left_new, right_new, moment):
@@ -274,16 +282,19 @@
         flops=2 * cube, moved=12 * area,
     )(l_parts, arrived)
     ready, norm = call(
-        right_kernel, (packed, jax.ShapeDtypeStruct((SUB, LANES), F32)), [vmem()] * 2, (vmem(),) * 2, "right",
+        right_kernel,
+        (jax.ShapeDtypeStruct((dp, ROWS, FOLDS * block), BF16), jax.ShapeDtypeStruct((SUB, LANES), F32)),
+        [vmem()] * 2, (vmem(),) * 2, "right",
         flops=3 * cube, moved=10 * area,
     )(half, r_parts)
     ready = call(
-        functools.partial(adam_kernel, limit, *grid), packed,
-        [vmem()] * 7 + [pl.BlockSpec(memory_space=pl.ANY)], tail, "adam",
-        moved=8 * area,
-        scratch_shapes=[pltpu.VMEM((LANES, LANES), F32)],
-        input_output_aliases={7: 0},
-        grid=(1,),
+        functools.partial(adam_kernel, limit, *grid), packed, [vmem()] * 8, hbm(), "adam",
+        moved=10 * area,
+        scratch_shapes=[
+            pltpu.VMEM((LANES, LANES), F32),
+            pltpu.VMEM((dp, ROWS, LANES), BF16),
+            pltpu.SemaphoreType.DMA((2,)),
+        ],
     )(grad, second, *sqs, norm, ready)
     returned = exchange(ready)
     left_new, right_new, moment = call(

time: 69.3 us -> 69.3 us (level)
  Pallas kernels: 13.3 us -> 12.4 us
  waiting for transfers between devices: 27.2 us -> 28 us
    ppermute x3, waiting for transfers between devices: 0.16 us -> 0.94 us  [swap(): return lax.ppermute(x, ('dp', 'expert'), pairs)]
    pallas_call x2, Pallas kernels: 3.68 us -> 2.9 us  [the longest x1 1.67 us: on_device(): call(functools.partial(adam_kernel, limit, *grid), packed, [vmem()] * 8,...]
  transfers between devices with their start and end apart: 5 -> 5, of which waited for: 3 -> 3; matrix products, arithmetic and copies ran while one was open for 0% -> 0% of each run, Pallas kernels for 12% -> 10%
where the time goes in v4:
time: 69.3 us; the launch traced here: 68.8 us
  waiting for transfers between devices  28 us (40%)
  starting transfers between devices  22.7 us (33%)
  Pallas kernels  12.4 us (18%)
  local copies, waits for them, and re-layouts  4.99 us (7%)
  between operations  0.75 us (1%)
    all_to_all x2, waiting for transfers between devices, exchange(): return lax.all_to_all(x, 'dp', split_axis=0, concat_axis=0, tiled=True)  27 us
    all_to_all x2, starting transfers between devices, exchange(): return lax.all_to_all(x, 'dp', split_axis=0, concat_axis=0, tiled=True)  18.7 us
    unnamed x18, local copies, waits for them, and re-layouts  4.99 us
    ppermute x3, starting transfers between devices, swap(): return lax.ppermute(x, ('dp', 'expert'), pairs)  3.94 us
    pallas_call x1, Pallas kernels, on_device(): call(functools.partial(finish_kernel, limit, dp, block, width // LANES),...  3.56 us
    pallas_call x1, Pallas kernels, on_device(): call(functools.partial(pack_kernel, *grid), packed, [hbm(), hbm()], hbm()...  2 us
    pallas_call x1, Pallas kernels, on_device(): call(functools.partial(adam_kernel, limit, *grid), packed, [vmem()] * 8,...  1.67 us
    pallas_call x1, Pallas kernels, on_device(): call(functools.partial(place_kernel, *grid), jax.ShapeDtypeStruct((local_...  1.5 us
  transfers between devices with their start and end apart: 5, of which 3 were waited for; matrix products, arithmetic and copies ran while one was open for 0% of the time, Pallas kernels for 10%

profile of v4, /device:TPU:1, one launch (start us, length us, event | category | flops | bytes accessed | tf_op | source)
XLA Modules:
  0.0 68.8 jit_solution(713006738938545141)
XLA Ops:
  0.6 2.0 %pack.1 = bf16[64,2,2176]{2,1,0:T(2,128)(2,1)} custom-call(s32[1,64]{1,0:T(1,128)} %owner_lanes.1, bf16[64,4096]{1,0:T(8,128)(2,1)} %bitcast.10), custom_call_target="tpu_custom_call" | custom-call | bytes 1048576 | tf_op jit(solution)/shard_map/pack/pallas_call | solution.py:261
  2.6 0.0 copy-start.5
  2.7 13.3 %all-to-all-start = ((bf16[64,2,2176]{2,1,0:T(2,128)(2,1)}), bf16[64,2,2176]{2,1,0:T(2,128)(2,1)S(1)}, u32[]{:S(2)}, u32[]{:S(2)}) async-start(bf16[64,2,2176]{2,1,0:T(2,128)(2,1)} %pack.1), calls=%async_computation | async-start | bytes 1114112 | tf_op jit(solution)/shard_map/all_to_all | solution.py:253
  16.0 0.0 copy-done.5
  16.0 0.0 copy-start.6
  16.0 1.2 %copy-done.6 = f32[1,1,512,512]{3,2,1,0:T(8,128)S(1)} copy-done((f32[1,1,512,512]{3,2,1,0:T(8,128)S(1)}, f32[1,1,512,512]{3,2,1,0:T(8,128)}, u32[]{:S(2)}) %copy-start.6) | copy-done | bytes 1048600
  17.2 1.5 %roots.1 = (bf16[2,512,512]{2,1,0:T(8,128)(2,1)S(1)}, bf16[2,512,512]{2,1,0:T(8,128)(2,1)S(1)}) custom-call(f32[512,512]{1,0:T(8,128)S(1)} %bitcast.17, f32[512,512]{1,0:T(8,128)S(1)} %bitcast.18), custom_call_target="tpu_custom_call" | custom-call | flops 1073741824 | bytes 4194304 | tf_op jit(solution)/shard_map/roots/pallas_call | solution.py:274
  18.7 0.0 copy-start.7
  18.7 1.0 %copy-done.7 = bf16[2,512,512]{2,1,0:T(8,128)(2,1)} copy-done((bf16[2,512,512]{2,1,0:T(8,128)(2,1)}, bf16[2,512,512]{2,1,0:T(8,128)(2,1)S(1)}, u32[]{:S(2)}) %copy-start.7) | copy-done | bytes 1048600
  19.7 14.7 %all-to-all-done.tiles.arrived = bf16[64,2,2176]{2,1,0:T(2,128)(2,1)S(1)} async-done(((bf16[64,2,2176]{2,1,0:T(2,128)(2,1)}), bf16[64,2,2176]{2,1,0:T(2,128)(2,1)S(1)}, u32[]{:S(2)}, u32[]{:S(2)}) %all-to-all-start) | async-done | bytes 557088 | tf_op jit(solution)/shard_map/all_to_all | solution.py:253
  34.3 0.1 norm.1.sq_0
  34.4 2.9 %collective-permute-start.2 = (f32[1,128]{1,0:T(1,128)S(1)}, f32[1,128]{1,0:T(1,128)S(1)}, u32[]{:S(2)}, u32[]{:S(2)}) collective-permute-start(f32[1,128]{1,0:T(1,128)S(1)} %norm.1.sq_0), channel_id=1, source_target_pairs={{0,7},{1,6},{2,5},{3,4},{4,3},{5,2},{6,1},{7,0},{8,15},{9,14},{10,... | collective-permute-start | bytes 1544 | tf_op jit(solution)/shard_map/ppermute | solution.py:259
  37.3 0.5 collective-permute-start.1
  37.8 0.6 collective-permute-start
  38.4 0.0 copy-start.8
  38.4 0.9 %left.1.half = f32[512,512]{1,0:T(8,128)S(1)} custom-call(bf16[2,512,512]{2,1,0:T(8,128)(2,1)S(1)} %get-tuple-element.11.l_parts, bf16[64,2,2176]{2,1,0:T(2,128)(2,1)S(1)} %all-to-all-done.tiles.arrived), custom_call_target="tpu_custom_call" | custom-call | flops 536870912 | bytes 3145728 | tf_op jit(solution)/shard_map/left/pallas_call | solution.py:280
  39.3 0.3 copy-done.8
  39.6 1.2 %right.1 = (bf16[64,2,2048]{2,1,0:T(2,128)(2,1)S(1)}, f32[8,128]{1,0:T(8,128)S(1)}) custom-call(f32[512,512]{1,0:T(8,128)S(1)} %left.1.half, bf16[2,512,512]{2,1,0:T(8,128)(2,1)S(1)} %copy-done.8), custom_call_target="tpu_custom_call" | custom-call | flops 805306368 | bytes 2621440 | tf_op jit(solution)/shard_map/right/pallas_call | solution.py:284
  40.9 0.0 collective-permute-done.2.sq_3
  40.9 0.9 %collective-permute-done.1.sq_2 = f32[1,128]{1,0:T(1,128)S(1)} collective-permute-done((f32[1,128]{1,0:T(1,128)S(1)}, f32[1,128]{1,0:T(1,128)S(1)}, u32[]{:S(2)}, u32[]{:S(2)}) %collective-permute-start.1) | collective-permute-done | bytes 544 | tf_op jit(solution)/shard_map/ppermute | solution.py:259
  41.8 0.0 collective-permute-done.sq_1
  41.8 0.0 copy-done
  41.8 0.0 copy-done.1
  41.8 1.7 %adam.1 = bf16[64,2,2176]{2,1,0:T(2,128)(2,1)} custom-call(bf16[64,4096]{1,0:T(8,128)(2,1)S(1)} %bitcast.11, f32[2048,128]{1,0:T(8,128)S(1)} %bitcast.13, f32[1,128]{1,0:T(1,128)S(1)} %norm.1.sq_0, f32[1,128]{1,0:T(1,128)S(1)} %collective-permute-done.sq_1, f32[1,128]{1,0:T(1,128)S(1)} %collective-permute-done.1.sq_2, ...), custom_call_target="tpu_custom_call" | custom-call | bytes 2621440 | tf_op jit(solution)/shard_map/adam/pallas_call | solution.py:290
  43.5 5.4 %all-to-all-start.1 = ((bf16[64,2,2176]{2,1,0:T(2,128)(2,1)}), bf16[64,2,2176]{2,1,0:T(2,128)(2,1)S(1)}, u32[]{:S(2)}, u32[]{:S(2)}) async-start(bf16[64,2,2176]{2,1,0:T(2,128)(2,1)} %adam.1), calls=%async_computation.1 | async-start | bytes 1114112 | tf_op jit(solution)/shard_map/all_to_all | solution.py:253
  48.9 0.0 copy-start.2
  48.9 1.2 %copy-done.2 = f32[1,1,512,512]{3,2,1,0:T(8,128)S(1)} copy-done((f32[1,1,512,512]{3,2,1,0:T(8,128)S(1)}, f32[1,1,512,512]{3,2,1,0:T(8,128)}, u32[]{:S(2)}) %copy-start.2) | copy-done | bytes 1048600
  50.2 1.2 %copy-done.3 = f32[1,1,512,512]{3,2,1,0:T(8,128)S(1)} copy-done((f32[1,1,512,512]{3,2,1,0:T(8,128)S(1)}, f32[1,1,512,512]{3,2,1,0:T(8,128)}, u32[]{:S(2)}) %copy-start.3) | copy-done | bytes 1048600
  51.4 3.6 %finish.1 = (f32[512,512]{1,0:T(8,128)}, f32[512,512]{1,0:T(8,128)}, f32[2048,128]{1,0:T(8,128)}) custom-call(bf16[64,2,2176]{2,1,0:T(2,128)(2,1)S(1)} %all-to-all-done.tiles.arrived, f32[1,128]{1,0:T(1,128)S(1)} %norm.1.sq_0, f32[1,128]{1,0:T(1,128)S(1)} %collective-permute-done.sq_1, f32[1,128]{1,0:T(1,128)S(1)} %collective-permute-done.1.sq_2, ...), custom_call_target="tpu_custom_call" | custom-call | flops 805306368 | bytes 7340032 | tf_op jit(solution)/shard_map/finish/pallas_call | solution.py:300
  54.9 12.4 %all-to-all-done.1.returned = bf16[64,2,2176]{2,1,0:T(2,128)(2,1)S(1)} async-done(((bf16[64,2,2176]{2,1,0:T(2,128)(2,1)}), bf16[64,2,2176]{2,1,0:T(2,128)(2,1)S(1)}, u32[]{:S(2)}, u32[]{:S(2)}) %all-to-all-start.1) | async-done | bytes 557088 | tf_op jit(solution)/shard_map/all_to_all | solution.py:253
  67.3 0.0 copy-done.4
  67.3 1.5 %place.1 = bf16[64,4096]{1,0:T(8,128)(2,1)} custom-call(s32[1,64]{1,0:T(1,128)S(1)} %copy-done.4, s32[1,64]{1,0:T(1,128)S(1)} %copy-done.4, bf16[64,2,2176]{2,1,0:T(2,128)(2,1)S(1)} %all-to-all-done.1.returned), custom_call_target="tpu_custom_call" | custom-call | bytes 1048576 | tf_op jit(solution)/shard_map/place/pallas_call | solution.py:306
  (4 shorter events, 0.0 us)
Async XLA Ops:
  2.6 13.3 %copy-start.5 = (f32[1,1,512,512]{3,2,1,0:T(8,128)S(1)}, f32[1,1,512,512]{3,2,1,0:T(8,128)}, u32[]{:S(2)}) copy-start(f32[1,1,512,512]{3,2,1,0:T(8,128)} %param.11) | copy-start | bytes 3145732
  2.7 31.7 %all-to-all-start = ((bf16[64,2,2176]{2,1,0:T(2,128)(2,1)}), bf16[64,2,2176]{2,1,0:T(2,128)(2,1)S(1)}, u32[]{:S(2)}, u32[]{:S(2)}) async-start(bf16[64,2,2176]{2,1,0:T(2,128)(2,1)} %pack.1), calls=%async_computation | async-start | bytes 1114112 | tf_op jit(solution)/shard_map/all_to_all | solution.py:253
  16.0 1.2 %copy-start.6 = (f32[1,1,512,512]{3,2,1,0:T(8,128)S(1)}, f32[1,1,512,512]{3,2,1,0:T(8,128)}, u32[]{:S(2)}) copy-start(f32[1,1,512,512]{3,2,1,0:T(8,128)} %param.12) | copy-start | bytes 3145732
  18.7 1.0 %copy-start.7 = (bf16[2,512,512]{2,1,0:T(8,128)(2,1)}, bf16[2,512,512]{2,1,0:T(8,128)(2,1)S(1)}, u32[]{:S(2)}) copy-start(bf16[2,512,512]{2,1,0:T(8,128)(2,1)S(1)} %get-tuple-element.12.r_parts) | copy-start | bytes 3145732
  34.4 6.4 %collective-permute-start.2 = (f32[1,128]{1,0:T(1,128)S(1)}, f32[1,128]{1,0:T(1,128)S(1)}, u32[]{:S(2)}, u32[]{:S(2)}) collective-permute-start(f32[1,128]{1,0:T(1,128)S(1)} %norm.1.sq_0), channel_id=1, source_target_pairs={{0,7},{1,6},{2,5},{3,4},{4,3},{5,2},{6,1},{7,0},{8,15},{9,14},{10,... | collective-permute-start | bytes 1544 | tf_op jit(solution)/shard_map/ppermute | solution.py:259
  37.3 4.5 %collective-permute-start.1 = (f32[1,128]{1,0:T(1,128)S(1)}, f32[1,128]{1,0:T(1,128)S(1)}, u32[]{:S(2)}, u32[]{:S(2)}) collective-permute-start(f32[1,128]{1,0:T(1,128)S(1)} %norm.1.sq_0), channel_id=1, source_target_pairs={{0,6},{1,7},{2,4},{3,5},{4,2},{5,3},{6,0},{7,1},{8,14},{9,15},{10,... | collective-permute-start | bytes 1544 | tf_op jit(solution)/shard_map/ppermute | solution.py:259
  37.8 4.0 %collective-permute-start = (f32[1,128]{1,0:T(1,128)S(1)}, f32[1,128]{1,0:T(1,128)S(1)}, u32[]{:S(2)}, u32[]{:S(2)}) collective-permute-start(f32[1,128]{1,0:T(1,128)S(1)} %norm.1.sq_0), channel_id=1, source_target_pairs={{0,5},{1,4},{2,7},{3,6},{4,1},{5,0},{6,3},{7,2},{8,13},{9,12},{10,... | collective-permute-start | bytes 1544 | tf_op jit(solution)/shard_map/ppermute | solution.py:259
  38.4 1.2 %copy-start.8 = (bf16[2,512,512]{2,1,0:T(8,128)(2,1)S(1)}, bf16[2,512,512]{2,1,0:T(8,128)(2,1)}, u32[]{:S(2)}) copy-start(bf16[2,512,512]{2,1,0:T(8,128)(2,1)} %copy-done.7) | copy-start | bytes 3145732
  39.6 2.2 %copy-start = (bf16[1,64,1,4096]{3,1,2,0:T(8,128)(2,1)S(1)}, bf16[1,64,1,4096]{3,1,2,0:T(8,128)(2,1)}, u32[]{:S(2)}) copy-start(bf16[1,64,1,4096]{3,1,2,0:T(8,128)(2,1)} %param.7) | copy-start | bytes 1572868
  39.6 2.2 %copy-start.1 = (f32[1,64,1,4096]{3,2,1,0:T(1,128)S(1)}, f32[1,64,1,4096]{3,2,1,0:T(1,128)}, u32[]{:S(2)}) copy-start(f32[1,64,1,4096]{3,2,1,0:T(1,128)} %param.8) | copy-start | bytes 3145732
  43.5 23.8 %all-to-all-start.1 = ((bf16[64,2,2176]{2,1,0:T(2,128)(2,1)}), bf16[64,2,2176]{2,1,0:T(2,128)(2,1)S(1)}, u32[]{:S(2)}, u32[]{:S(2)}) async-start(bf16[64,2,2176]{2,1,0:T(2,128)(2,1)} %adam.1), calls=%async_computation.1 | async-start | bytes 1114112 | tf_op jit(solution)/shard_map/all_to_all | solution.py:253
  48.9 1.2 %copy-start.2 = (f32[1,1,512,512]{3,2,1,0:T(8,128)S(1)}, f32[1,1,512,512]{3,2,1,0:T(8,128)}, u32[]{:S(2)}) copy-start(f32[1,1,512,512]{3,2,1,0:T(8,128)} %param.9) | copy-start | bytes 3145732
  50.2 1.2 %copy-start.3 = (f32[1,1,512,512]{3,2,1,0:T(8,128)S(1)}, f32[1,1,512,512]{3,2,1,0:T(8,128)}, u32[]{:S(2)}) copy-start(f32[1,1,512,512]{3,2,1,0:T(8,128)} %param.10) | copy-start | bytes 3145732
  51.4 15.9 %copy-start.4 = (s32[1,64]{1,0:T(1,128)S(1)}, s32[1,64]{1,0:T(1,128)}, u32[]{:S(2)}) copy-start(s32[1,64]{1,0:T(1,128)} %owner_lanes.1) | copy-start | bytes 772
